TPU v7x, 32 devices: a whole 2x2x4 slice. The times are simulated.
32 devices in a mesh: tm: 8 (over z, x), space: 4 (over y, core).
Axes of the slice: x: 2, y: 2, z: 4, core: 2. Of those that a mesh axis runs over, the one named last changes fastest.
Arguments:
- start_block: float32 [8, 2, 3, 32, 32, 256], P('tm', None, None, None, 'space'), may hold values from -6 to 6
- gauge_links: float32 [8, 3, 2, 3, 3, 32, 256], P('tm', None, None, None, None, 'space'), may hold values from -1 to 1, as said below
- stored_vectors: bfloat16 [8, 448, 2, 3, 32, 256], P('tm', None, None, None, 'space'), may hold values from -0.02734375 to 0.02734375
Outputs:
- correlations: float32 [8, 448, 64], P('tm', 'space')
- solver_blocks: bfloat16 [8, 32, 256, 192], P('space', None, 'tm')
Inputs may be any that keep to these rules, and one draw needn't show every extreme that they name: Every link matrix gauge_links[t, mu, 0] + i gauge_links[t, mu, 1] at a site is special unitary, drawn independently at every site and direction.
All inputs are finite; a program needn't handle non-finite values.
Results may differ from a plain program's by a relative error of at most 0.0029.
Values may be sent and summed in bfloat16 or wider, within the bound.
No kernel may reach another device: no remote copies, remote signals or barrier semaphores. Data moves between devices by JAX's collectives and lax.ppermute only.
A program may use at most 128 MiB of HBM per device.

v0:
```python
import functools

import jax
import jax.numpy as jnp
from jax import lax
from jax.experimental import pallas as pl
from jax.experimental.pallas import tpu as pltpu
from jax.sharding import PartitionSpec as P

DEGREE = 4
LZ = 16
LANES = 128
VB = 16

lower_edge = 0.5
upper_edge = 12.5
SCALE = 2.0 / (upper_edge - lower_edge)
OFFSET = (upper_edge + lower_edge) / (upper_edge - lower_edge)

VMEM_LIMIT = 60 * 2**20
LINK_ROWS = 54
LINK_PAD = 56
TABLE_ROWS = 112
GAUGE_ROWS = 24


def params(limit=24 * 2**20):
    return pltpu.CompilerParams(vmem_limit_bytes=limit)


def in_vmem(count):
    return [pl.BlockSpec(memory_space=pltpu.VMEM)] * count


def in_smem():
    return pl.BlockSpec(memory_space=pltpu.SMEM)


def cost(microseconds):
    return pl.CostEstimate(
        flops=1_000_000, bytes_accessed=int(microseconds * 3_000_000), transcendentals=0
    )


def fetch(start_hbm, links_hbm, start_ref, links_ref, sems):
    comps = start_ref.shape[0]
    copies = [pltpu.make_async_copy(links_hbm, links_ref, sems.at[comps])] + [
        pltpu.make_async_copy(start_hbm.at[k], start_ref.at[k], sems.at[k]) for k in range(comps)
    ]
    for copy in copies:
        copy.start()
    return copies


def fetch_scratch(start2, links2):
    return [
        pltpu.VMEM(start2.shape, jnp.float32),
        pltpu.VMEM(links2.shape, jnp.float32),
        pltpu.SemaphoreType.DMA((start2.shape[0] + 1,)),
    ]


def pack_kernel(
    start_hbm, links_hbm, up_links_ref, down_links_ref, up_ref, down_ref,
    start_ref, links_ref, sems, *, layers, tiles
):
    comps, groups = up_ref.shape[2], up_ref.shape[1]
    cells = VB * layers * tiles
    copies = fetch(start_hbm, links_hbm, start_ref, links_ref, sems)
    copies[0].wait()
    for x in range(layers):
        for t in range(tiles):
            rows = links_ref[pl.ds(t * layers + x, LINK_ROWS, stride=tiles * layers), :]
            if x < DEGREE:
                down_links_ref[x, :, cols(t)] = rows.astype(jnp.bfloat16)
            if x >= layers - DEGREE:
                up_links_ref[x - layers + DEGREE, :, cols(t)] = rows.astype(jnp.bfloat16)
    for k in range(comps):
        copies[1 + k].wait()
        for x in range(layers):
            for t in range(tiles):
                for g in range(groups):
                    half = start_ref[
                        k, pl.ds(g * cells + t * layers + x, VB, stride=tiles * layers), :
                    ].astype(jnp.bfloat16)
                    if x < DEGREE:
                        down_ref[x, g, k, :, cols(t)] = half
                    if x >= layers - DEGREE:
                        up_ref[x - layers + DEGREE, g, k, :, cols(t)] = half


def run_pack(start2, links2, layers, tiles):
    comps, rows, _ = start2.shape
    planes = tiles * LANES
    groups = rows // (VB * layers * tiles)
    link = jax.ShapeDtypeStruct((DEGREE, LINK_ROWS, planes), jnp.bfloat16)
    halo = jax.ShapeDtypeStruct((DEGREE, groups, comps, VB, planes), jnp.bfloat16)
    return pl.pallas_call(
        functools.partial(pack_kernel, layers=layers, tiles=tiles),
        in_specs=[pl.BlockSpec(memory_space=pltpu.HBM)] * 2,
        out_specs=in_vmem(4),
        out_shape=[link, link, halo, halo],
        scratch_shapes=fetch_scratch(start2, links2),
        compiler_params=params(VMEM_LIMIT),
        cost_estimate=cost(2.5),
        name="pack",
    )(start2, links2)


def mat_mul(a, b, conj_b=False):
    out_re, out_im = [], []
    for i in range(3):
        for j in range(3):
            re = im = None
            for k in range(3):
                ar, ai = a[0][3 * i + k], a[1][3 * i + k]
                if conj_b:
                    br, bi = b[0][3 * j + k], b[1][3 * j + k]
                    r = ar * br + ai * bi
                    m = ai * br - ar * bi
                else:
                    br, bi = b[0][3 * k + j], b[1][3 * k + j]
                    r = ar * br - ai * bi
                    m = ar * bi + ai * br
                re = r if re is None else re + r
                im = m if im is None else im + m
            out_re.append(re)
            out_im.append(im)
    return out_re, out_im


def rot(v, steps):
    return pltpu.roll(v, steps % LANES, 1)


def shifts(value, masks):
    z_last, z_first, y_low, y_high = masks
    tiles = len(value)
    up = [rot(v, LZ) for v in value]
    down = [rot(v, -LZ) for v in value]
    return (
        [jnp.where(y_low, down[t], down[(t + 1) % tiles]) for t in range(tiles)],
        [jnp.where(y_high, up[t], up[(t - 1) % tiles]) for t in range(tiles)],
        [rot(jnp.where(z_first, up[t], value[t]), -1) for t in range(tiles)],
        [rot(jnp.where(z_last, down[t], value[t]), 1) for t in range(tiles)],
    )


def lane_masks(rows):
    lane = lax.broadcasted_iota(jnp.int32, (rows, LANES), 1)
    return lane % LZ == LZ - 1, lane % LZ == 0, lane < LANES - LZ, lane >= LZ


def cols(t):
    return slice(t * LANES, (t + 1) * LANES)


def rows_at(ref, t, first):
    return (
        [ref[t, pl.ds(first + k, 1), :] for k in range(9)],
        [ref[t, pl.ds(first + 9 + k, 1), :] for k in range(9)],
    )


def put_rows(ref, t, first, g):
    for k in range(9):
        ref[t, pl.ds(first + k, 1), :] = g[0][k]
        ref[t, pl.ds(first + 9 + k, 1), :] = g[1][k]


def unit_rows():
    one = jnp.ones((1, LANES), jnp.float32)
    zero = jnp.zeros((1, LANES), jnp.float32)
    return [one if k % 4 == 0 else zero for k in range(9)], [zero] * 9


def fill_tables(ext_ref, g_ref, t_ref, table_ref, gauge_ref, places):
    tiles = ext_ref.shape[0]
    total = len(places)
    masks = lane_masks(total)

    def column(ref, k, stride):
        return [ref[t, pl.ds(k, total, stride=stride), :] for t in range(tiles)]

    gauge = [column(g_ref, k, GAUGE_ROWS) for k in range(18)]
    for d in (1, 2):
        link = [column(ext_ref, 18 * d + k, LINK_PAD) for k in range(18)]
        ahead = [shifts(v, masks)[2 * (d - 1)] for v in gauge]
        turned = []
        for t in range(tiles):
            here, there, mid = (
                ([v[t] for v in field[:9]], [v[t] for v in field[9:]])
                for field in (gauge, ahead, link)
            )
            turned.append(mat_mul(mat_mul(here, mid), there, conj_b=True))
        base = 54 * (d - 1)
        for k in range(9):
            re, im = [turned[t][0][k] for t in range(tiles)], [turned[t][1][k] for t in range(tiles)]
            back_re, back_im = shifts(re, masks)[2 * d - 1], shifts(im, masks)[2 * d - 1]
            for t in range(tiles):
                for at, value in (
                    (0, re[t]),
                    (9, re[t] + im[t]),
                    (18, im[t] - re[t]),
                    (27, back_re[t]),
                    (36, back_re[t] + back_im[t]),
                    (45, back_im[t] - back_re[t]),
                ):
                    t_ref[t, pl.ds(base + at + k, total, stride=TABLE_ROWS), :] = value
    for n, x in enumerate(places):
        for t in range(tiles):
            table_ref[x, 0:108, cols(t)] = t_ref[t, pl.ds(n * TABLE_ROWS, 108), :]
            gauge_ref[x, 0:18, cols(t)] = g_ref[t, pl.ds(n * GAUGE_ROWS, 18), :]


def gauge_own(links_ref, table_ref, gauge_ref, ext_ref, g_ref, t_ref, layers):
    tiles = ext_ref.shape[0]
    for t in range(tiles):
        for x in range(layers):
            ext_ref[t, pl.ds(x * LINK_PAD, LINK_ROWS), :] = links_ref[
                pl.ds(t * layers + x, LINK_ROWS, stride=tiles * layers), :
            ]
    for t in range(tiles):
        g = unit_rows()
        put_rows(g_ref, t, 0, g)
        for x in range(layers - 1):
            g = mat_mul(g, rows_at(ext_ref, t, x * LINK_PAD))
            put_rows(g_ref, t, (x + 1) * GAUGE_ROWS, g)
    fill_tables(
        ext_ref, g_ref, t_ref, table_ref, gauge_ref, [DEGREE + x for x in range(layers)]
    )


def gauge_halo_kernel(
    top_ref, lo_ref, hi_ref, table_in, gauge_in, table_ref, gauge_ref, ext_ref, g_ref, t_ref
):
    layers = table_ref.shape[0] - 2 * DEGREE
    for x in range(DEGREE, DEGREE + layers):
        table_ref[x] = table_in[x]
        gauge_ref[x] = gauge_in[x]
    tiles = ext_ref.shape[0]
    for t in range(tiles):
        for x in range(DEGREE):
            ext_ref[t, pl.ds(x * LINK_PAD, LINK_ROWS), :] = lo_ref[x, :, cols(t)].astype(jnp.float32)
            ext_ref[t, pl.ds((DEGREE + x) * LINK_PAD, LINK_ROWS), :] = hi_ref[x, :, cols(t)].astype(
                jnp.float32
            )
    for t in range(tiles):
        g = unit_rows()
        for x in range(DEGREE - 1, -1, -1):
            g = mat_mul(g, rows_at(ext_ref, t, x * LINK_PAD), conj_b=True)
            put_rows(g_ref, t, x * GAUGE_ROWS, g)
        top = DEGREE + layers - 1
        g = tuple(
            [gauge_in[top, pl.ds(first + k, 1), cols(t)] for k in range(9)] for first in (0, 9)
        )
        link = tuple(
            [top_ref[pl.ds(first + k, 1), cols(t)] for k in range(9)]
            for first in (0, 9)
        )
        for x in range(DEGREE):
            g = mat_mul(g, link)
            put_rows(g_ref, t, (DEGREE + x) * GAUGE_ROWS, g)
            if x < DEGREE - 1:
                link = rows_at(ext_ref, t, (DEGREE + x) * LINK_PAD)
    places = list(range(DEGREE)) + [DEGREE + layers + x for x in range(DEGREE)]
    fill_tables(ext_ref, g_ref, t_ref, table_ref, gauge_ref, places)


def gauge_scratch(count, tiles):
    return [
        pltpu.VMEM((tiles, count * LINK_PAD, LANES), jnp.float32),
        pltpu.VMEM((tiles, count * GAUGE_ROWS, LANES), jnp.float32),
        pltpu.VMEM((tiles, count * TABLE_ROWS, LANES), jnp.float32),
    ]


def gauge_shapes(layers, planes):
    total = layers + 2 * DEGREE
    return [
        jax.ShapeDtypeStruct((total, TABLE_ROWS, planes), jnp.float32),
        jax.ShapeDtypeStruct((total, GAUGE_ROWS, planes), jnp.float32),
    ]


def gauge_halo(top, lo, hi, table, gauge):
    total, _, planes = table.shape
    return pl.pallas_call(
        gauge_halo_kernel,
        in_specs=in_vmem(5),
        out_specs=in_vmem(2),
        out_shape=gauge_shapes(total - 2 * DEGREE, planes),
        scratch_shapes=gauge_scratch(2 * DEGREE, planes // LANES),
        compiler_params=params(),
        cost_estimate=cost(1.5),
        name="gauge_halo",
    )(top, lo, hi, table, gauge)


def turn(gauge_ref, x, source, adjoint, tiles):
    out = {}
    for t in range(tiles):
        v = [source(k, t) for k in range(6)]
        for i in range(3):
            re = im = None
            for j in range(3):
                k = 3 * j + i if adjoint else 3 * i + j
                a = gauge_ref[x, pl.ds(k, 1), cols(t)]
                b = gauge_ref[x, pl.ds(9 + k, 1), cols(t)]
                if adjoint:
                    r, m = a * v[j] + b * v[3 + j], a * v[3 + j] - b * v[j]
                else:
                    r, m = a * v[j] - b * v[3 + j], a * v[3 + j] + b * v[j]
                re = r if re is None else re + r
                im = m if im is None else im + m
            out[i, t], out[3 + i, t] = re, im
    return out


def layer(table_ref, g, x, src, prev, first, tiles):
    z_last, z_first, y_low, y_high = lane_masks(VB)
    sums = {}

    def add(key, value, minus=False):
        have = sums.get(key)
        if have is None:
            sums[key] = -value if minus else value
        else:
            sums[key] = have - value if minus else have + value

    def hop(t, base, v, adjoint):
        both = [v[j] + v[3 + j] for j in range(3)]
        for j in range(3):
            for i in range(3):
                k = base + (3 * j + i if adjoint else 3 * i + j)
                a = table_ref[x, pl.ds(k, 1), cols(t)]
                p = table_ref[x, pl.ds(k + 9, 1), cols(t)]
                q = table_ref[x, pl.ds(k + 18, 1), cols(t)]
                add((t, 0, i), a * both[j])
                if adjoint:
                    add((t, 1, i), q * v[3 + j], True)
                    add((t, 2, i), p * v[j], True)
                else:
                    add((t, 1, i), p * v[3 + j])
                    add((t, 2, i), q * v[j])

    out = {}
    for t in range(tiles):
        c = {(k, u): src[g, x, k, :, cols(u)] for k in range(6) for u in range(tiles)}
        after, before = (t + 1) % tiles, (t - 1) % tiles
        hop(t, 0, [rot(jnp.where(y_high, c[k, t], c[k, after]), -LZ) for k in range(6)], False)
        hop(t, 27, [rot(jnp.where(y_low, c[k, t], c[k, before]), LZ) for k in range(6)], True)
        hop(
            t, 54,
            [jnp.where(z_last, rot(c[k, t], LZ - 1), rot(c[k, t], -1)) for k in range(6)],
            False,
        )
        hop(
            t, 81,
            [jnp.where(z_first, rot(c[k, t], 1 - LZ), rot(c[k, t], 1)) for k in range(6)],
            True,
        )
        for i in range(3):
            re = sums[t, 0, i] - sums[t, 1, i]
            im = sums[t, 0, i] + sums[t, 2, i]
            for k, h in ((i, re), (3 + i, im)):
                h = h + (src[g, x + 1, k, :, cols(t)] + src[g, x - 1, k, :, cols(t)])
                if first:
                    out[k, t] = (6.0 * SCALE - OFFSET) * c[k, t] - SCALE * h
                else:
                    out[k, t] = (
                        (12.0 * SCALE - 2.0 * OFFSET) * c[k, t]
                        - (2.0 * SCALE) * h
                        - prev[g, x, k, :, cols(t)]
                    )
    return out


def put(ref, g, x, values):
    for (k, t), value in values.items():
        ref[g, x, k, :, cols(t)] = value


def inner_kernel(
    start_hbm, links_hbm, a_ref, b_ref, table_ref, gauge_ref, top_ref,
    start_ref, links_ref, sems, ext_ref, g_ref, t_ref, *, layers
):
    groups = a_ref.shape[0]
    tiles = table_ref.shape[-1] // LANES
    cells = VB * layers * tiles
    copies = fetch(start_hbm, links_hbm, start_ref, links_ref, sems)
    copies[0].wait()
    gauge_own(links_ref, table_ref, gauge_ref, ext_ref, g_ref, t_ref, layers)
    for t in range(tiles):
        top_ref[0:18, cols(t)] = ext_ref[t, pl.ds((layers - 1) * LINK_PAD, 18), :]
    for copy in copies[1:]:
        copy.wait()

    def init(n, _):
        g, x = n // layers, n % layers

        def source(k, t):
            at = g * cells + t * layers + x
            return start_ref[k, pl.ds(at, VB, stride=tiles * layers), :]

        put(a_ref, g, x + DEGREE, turn(gauge_ref, x + DEGREE, source, False, tiles))
        return 0

    lax.fori_loop(0, groups * layers, init, 0)
    for level in range(1, DEGREE):
        src, dst = (a_ref, b_ref) if level % 2 else (b_ref, a_ref)
        pairs = (layers - 2 * level) // 2

        def body(n, _, src=src, dst=dst, level=level, pairs=pairs):
            g, at = n // pairs, n % pairs
            for u in range(2):
                x = DEGREE + level + 2 * at + u
                put(dst, g, x, layer(table_ref, g, x, src, dst, level == 1, tiles))
            return 0

        if pairs > 0:
            lax.fori_loop(0, groups * pairs, body, 0)


def run_inner(start2, links2, layers, tiles):
    comps, rows, _ = start2.shape
    planes = tiles * LANES
    groups = rows // (VB * layers * tiles)
    state = jax.ShapeDtypeStruct((groups, layers + 2 * DEGREE, comps, VB, planes), jnp.float32)
    top = jax.ShapeDtypeStruct((GAUGE_ROWS, planes), jnp.float32)
    return pl.pallas_call(
        functools.partial(inner_kernel, layers=layers),
        in_specs=[pl.BlockSpec(memory_space=pltpu.HBM)] * 2,
        out_specs=in_vmem(5),
        out_shape=[state, state] + gauge_shapes(layers, planes) + [top],
        scratch_shapes=fetch_scratch(start2, links2) + gauge_scratch(layers, tiles),
        compiler_params=params(),
        cost_estimate=cost(8),
        name="inner",
    )(start2, links2)


def outer_kernel(
    place_ref, lo_ref, hi_ref, table_ref, gauge_ref, a_in, b_in,
    half_ref, keep_ref, give_ref, a_ref, b_ref, pack_ref, *, layers, parts
):
    groups = a_ref.shape[0]
    total = layers + 2 * DEGREE
    planes = table_ref.shape[-1]
    tiles = planes // LANES

    def init(n, _):
        g, x = n // DEGREE, n % DEGREE
        for ref, at in ((lo_ref, x), (hi_ref, x + DEGREE + layers)):

            def source(k, t, ref=ref):
                return ref[x, g, k, :, cols(t)].astype(jnp.float32)

            put(a_ref, g, at, turn(gauge_ref, at, source, False, tiles))
        for at in (x + DEGREE, total - 2 * DEGREE + x):
            a_ref[g, at] = a_in[g, at]
            b_ref[g, at] = b_in[g, at]
        return 0

    lax.fori_loop(0, groups * DEGREE, init, 0)
    for level in range(1, DEGREE):
        src, dst = (a_ref, b_ref) if level % 2 else (b_ref, a_ref)

        def body(n, _, src=src, dst=dst, level=level):
            g, at = n // DEGREE, n % DEGREE
            for x in (level + at, total - DEGREE - level + at):
                put(dst, g, x, layer(table_ref, g, x, src, dst, level == 1, tiles))
            return 0

        lax.fori_loop(0, groups * DEGREE, body, 0)
    src, prev = (a_ref, b_ref) if DEGREE % 2 else (b_ref, a_ref)

    def last(n, _):
        g, at = n // (layers // 2), n % (layers // 2)
        for u in range(2):
            x = 2 * at + u
            value = layer(table_ref, g, x + DEGREE, src, prev, False, tiles)
            value = turn(gauge_ref, x + DEGREE, lambda k, t: value[k, t], True, tiles)
            for (k, t), v in value.items():
                rounded = v.astype(jnp.bfloat16)
                half_ref[g, x, k, :, cols(t)] = rounded
                pack_ref[g, k, pl.ds(pl.multiple_of(x * VB, VB), VB), cols(t)] = rounded.astype(
                    jnp.float32
                )
        return 0

    lax.fori_loop(0, groups * (layers // 2), last, 0)

    me, shift = place_ref[0], place_ref[1]
    pairs = parts // 2
    width = planes // parts
    for g in range(groups):
        for k in range(6):
            turned = jnp.concatenate([pack_ref[g, k, :, cols(t)].T for t in range(tiles)], axis=0)
            for m in range(pairs):
                even = turned[2 * m * width : (2 * m + 1) * width].astype(jnp.bfloat16)
                odd = turned[(2 * m + 1) * width : (2 * m + 2) * width].astype(jnp.bfloat16)
                at = lax.rem(m - shift + pairs, pairs)
                keep_ref[at, g, k] = jnp.where(me == 0, even, odd)
                give_ref[at, g, k] = jnp.where(me == 0, odd, even)


def run_outer(place, lo, hi, table, gauge, a, b, layers, parts):
    groups, total, comps, _, planes = a.shape
    width = planes // parts
    cells = layers * VB
    block = jax.ShapeDtypeStruct((parts // 2, groups, comps, width, cells), jnp.bfloat16)
    half = jax.ShapeDtypeStruct((groups, layers, comps, VB, planes), jnp.bfloat16)
    return pl.pallas_call(
        functools.partial(outer_kernel, layers=layers, parts=parts),
        in_specs=[in_smem()] + in_vmem(6),
        out_specs=in_vmem(3),
        out_shape=[half, block, block],
        scratch_shapes=[
            pltpu.VMEM(a.shape, jnp.float32),
            pltpu.VMEM(a.shape, jnp.float32),
            pltpu.VMEM((groups, comps, cells, planes), jnp.float32),
        ],
        compiler_params=params(),
        cost_estimate=cost(16),
        name="outer",
    )(place, lo, hi, table, gauge, a, b)


def weight_kernel(half_ref, weight_ref):
    groups, layers, _, _, planes = half_ref.shape
    vectors = groups * VB
    for g in range(groups):
        for x in range(layers):
            for part in range(2):
                for c in range(3):
                    for p in range(2):
                        value = half_ref[g, x, (part ^ p) * 3 + c]
                        if p == 1 and part == 1:
                            value = -value
                        weight_ref[
                            pl.ds((x * 2 + p) * vectors + g * VB, VB),
                            pl.ds((part * 3 + c) * planes, planes),
                        ] = value


def run_weights(half):
    groups, layers, comps, _, planes = half.shape
    return pl.pallas_call(
        weight_kernel,
        in_specs=in_vmem(1),
        out_specs=in_vmem(1)[0],
        out_shape=jax.ShapeDtypeStruct((layers * 2 * groups * VB, comps * planes), jnp.bfloat16),
        compiler_params=params(),
        cost_estimate=cost(0.7),
        name="weights",
    )(half)


def corr_kernel(place_ref, stored_ref, weight_ref, out_ref, *, layers):
    span, block = out_ref.shape
    _, comps, _, planes = stored_ref.shape
    rows = jnp.concatenate(
        [stored_ref[:, k].reshape(block * layers, planes) for k in range(comps)], axis=1
    )
    full = lax.dot_general(
        rows, weight_ref[...], (((1,), (1,)), ((), ())), preferred_element_type=jnp.float32
    )
    layer_of_row = lax.broadcasted_iota(jnp.int32, (block * layers, span), 0) % layers
    kept = jnp.zeros((block * layers, span), jnp.float32)
    for x in range(layers):
        kept = jnp.where(layer_of_row == x, full[:, x * span : (x + 1) * span], kept)
    out_ref[...] = jnp.sum(kept.reshape(block, layers, span), axis=1).T


def run_corr(place, stored, weights, owners):
    count, comps, layers, planes = stored.shape
    block = count // owners
    span = weights.shape[0] // layers
    grid_spec = pltpu.PrefetchScalarGridSpec(
        num_scalar_prefetch=1,
        grid=(owners,),
        in_specs=[
            pl.BlockSpec((block, comps, layers, planes), lambda g, s: (g, 0, 0, 0)),
            pl.BlockSpec(memory_space=pltpu.VMEM),
        ],
        out_specs=pl.BlockSpec((pl.Squeezed(), span, block), lambda g, s: (g ^ s[2], 0, 0)),
    )
    return pl.pallas_call(
        functools.partial(corr_kernel, layers=layers),
        grid_spec=grid_spec,
        out_shape=jax.ShapeDtypeStruct((owners, span, block), jnp.float32),
        compiler_params=params(40 * 2**20),
        cost_estimate=cost(11),
        name="correlate",
    )(place, stored, weights)


def merge_kernel(keep_ref, got_ref, *out_refs):
    for step, ref in enumerate(out_refs):
        ref[0] = keep_ref[step]
        ref[1] = got_ref[step]


def run_merge(keep, got):
    shape = jax.ShapeDtypeStruct((2,) + keep.shape[1:], keep.dtype)
    return pl.pallas_call(
        merge_kernel,
        in_specs=in_vmem(2),
        out_specs=in_vmem(keep.shape[0]),
        out_shape=[shape] * keep.shape[0],
        compiler_params=params(),
        cost_estimate=cost(0.7),
        name="merge",
    )(keep, got)


def order_kernel(order_ref, *, layers, groups):
    depth = order_ref.shape[0]
    cells = layers * VB
    vectors = groups * VB
    row = lax.broadcasted_iota(jnp.int32, (depth, depth), 0)
    col = lax.broadcasted_iota(jnp.int32, (depth, depth), 1)
    bit, rest = row // (groups * cells), row % (groups * cells)
    group, cell = rest // cells, rest % cells
    wanted = ((cell // VB) * 2 + bit) * vectors + group * VB + cell % VB
    order_ref[...] = (wanted == col).astype(jnp.bfloat16)


def run_order(groups, layers):
    depth = 2 * groups * layers * VB
    return pl.pallas_call(
        functools.partial(order_kernel, layers=layers, groups=groups),
        out_specs=in_vmem(1)[0],
        out_shape=jax.ShapeDtypeStruct((depth, depth), jnp.bfloat16),
        compiler_params=params(),
        cost_estimate=cost(2),
        name="order",
    )()


def arrange_kernel(place_ref, order_ref, *refs, layers):
    out_ref = refs[-1]
    groups, comps, width = refs[0].shape[1:4]
    span = 2 * groups * VB
    side = place_ref[4]

    def move(block_ref):
        for h in range(2):
            core = side if h == 0 else 1 - side
            pieces = []
            for pair in range(comps // 2):
                lanes = [
                    block_ref[h, g, 2 * pair + bit] for bit in range(2) for g in range(groups)
                ]
                pieces.append(jnp.concatenate(lanes, axis=1))
            moved = jnp.dot(
                jnp.concatenate(pieces, axis=0), order_ref[...], preferred_element_type=jnp.float32
            )
            for x in range(layers):
                out_ref[core * layers + x] = jnp.concatenate(
                    [
                        moved[p * width : (p + 1) * width, x * span : (x + 1) * span]
                        for p in range(comps // 2)
                    ],
                    axis=1,
                ).astype(jnp.bfloat16)

    for step, ref in enumerate(refs[:-1]):
        pl.when(pl.program_id(0) == step)(functools.partial(move, ref))


def run_arrange(place, order, blocks, shape, layers, near):
    pairs = len(blocks)

    def where(g, s):
        source = lax.rem(s[3] - g + pairs, pairs)
        return source // near, lax.rem(source, near), 0, 0

    grid_spec = pltpu.PrefetchScalarGridSpec(
        num_scalar_prefetch=1,
        grid=(pairs,),
        in_specs=in_vmem(1 + pairs),
        out_specs=pl.BlockSpec((pl.Squeezed(), 2 * layers) + shape[2:], where),
    )
    return pl.pallas_call(
        functools.partial(arrange_kernel, layers=layers),
        grid_spec=grid_spec,
        out_shape=jax.ShapeDtypeStruct(shape, jnp.bfloat16),
        compiler_params=params(),
        cost_estimate=cost(3),
        name="arrange",
    )(place, order, *blocks)


def shards(start_block, gauge_links, stored_vectors, *, n_tm, n_space):
    _, parts, colours, vectors, layers, planes = start_block.shape
    comps = parts * colours
    tm, space = lax.axis_index("tm"), lax.axis_index("space")
    per = n_tm // n_space
    near = n_space // 2
    pairs = n_tm // 2
    groups = vectors // VB
    core = lax.rem(space, 2)
    place = jnp.stack(
        [core, lax.rem(tm, per) * near + space // 2, space, tm // 2, lax.rem(tm, 2)]
    ).astype(jnp.int32)

    tiles = planes // LANES

    def by_tile(value, *lead):
        value = value.reshape(-1, layers, tiles, LANES)
        return jnp.transpose(value, (0, 2, 1, 3)).reshape(*lead, LANES)

    start2 = by_tile(start_block, comps, vectors * tiles * layers)
    links2 = by_tile(gauge_links, LINK_ROWS * tiles * layers)
    up = [(i, (i + 1) % n_space) for i in range(n_space)]
    down = [((i + 1) % n_space, i) for i in range(n_space)]

    up_links, down_links, up_halo, down_halo = run_pack(start2, links2, layers, tiles)
    lo_links = lax.ppermute(up_links, "space", up)
    hi_links = lax.ppermute(down_links, "space", down)
    lo = lax.ppermute(up_halo, "space", up)
    hi = lax.ppermute(down_halo, "space", down)
    order = run_order(groups, layers)

    a, b, table, gauge, top = run_inner(start2, links2, layers, tiles)
    table, gauge = gauge_halo(top, lo_links, hi_links, table, gauge)
    half, keep, give = run_outer(place, lo, hi, table, gauge, a, b, layers, n_tm)

    weights = run_weights(half)
    got = lax.ppermute(give, "space", [(i, i ^ 1) for i in range(n_space)])
    blocks = run_merge(keep, got)
    stored = stored_vectors.reshape(stored_vectors.shape[1], comps, layers, planes)
    sent = []
    for step, block in enumerate(blocks):
        table_of = []
        for i in range(n_tm):
            for j in range(n_space):
                m = ((i % per) * near + j // 2 + step) % pairs
                table_of.append((i * n_space + j, (2 * m + j % 2) * n_space + i // per))
        sent.append(lax.ppermute(block, ("tm", "space"), table_of))
    partial = run_corr(place, stored, weights, n_space)
    sums = {d: partial[d] for d in range(n_space)}

    bit = 1
    while bit < n_space:
        going = [d for d in sums if d & bit]
        partner = [(i, i ^ bit) for i in range(n_space)]
        came = lax.ppermute(jnp.stack([sums[d] for d in going]), "space", partner)
        for n, d in enumerate(going):
            sums[d ^ bit] = sums[d ^ bit] + came[n]
            del sums[d]
        bit *= 2
    correlations = sums[0].T[None]

    shape = (per, n_space * layers, planes // n_tm, comps * vectors)
    return correlations, run_arrange(place, order, sent, shape, layers, near)


def solution(mesh):
    in_specs = (
        P("tm", None, None, None, "space", None),
        P("tm", None, None, None, None, "space", None),
        P("tm", None, None, None, "space", None),
    )
    out_specs = (P("tm", "space", None), P("space", None, "tm", None))
    body = functools.partial(shards, n_tm=mesh.shape["tm"], n_space=mesh.shape["space"])
    return jax.shard_map(body, mesh=mesh, in_specs=in_specs, out_specs=out_specs, check_vma=False)
```

profile of v0, /device:TPU:12, one launch (start us, length us, event | category | flops | bytes accessed | tf_op | source)
XLA Modules:
  0.0 80.5 jit_solution(7976541213204642097)
XLA Ops:
  0.6 2.8 %pack.1 = (bf16[4,54,256]{2,1,0:T(8,128)(2,1)}, bf16[4,54,256]{2,1,0:T(8,128)(2,1)}, bf16[4,2,6,16,256]{4,3,2,1,0:T(8,128)(2,1)}, bf16[4,2,6,16,256]{4,3,2,1,0:T(8,128)(2,1)}) custom-call(f32[6,512,128]{2,1,0:T(8,128)} %bitcast.23, f32[864,128]{1,0:T(8,128)} %bitcast.25), custom_call_target="tpu_custom_call" | custom-call | flops 1000000 | bytes 7500000 | tf_op jit(solution)/shard_map/pack/pallas_call | solution.py:98
  3.6 1.7 %collective-permute-start.1 = (bf16[4,2,6,16,256]{4,3,2,1,0:T(8,128)(2,1)}, bf16[4,2,6,16,256]{4,3,2,1,0:T(8,128)(2,1)S(1)}, u32[]{:S(2)}, u32[]{:S(2)}) collective-permute-start(bf16[4,2,6,16,256]{4,3,2,1,0:T(8,128)(2,1)} %get-tuple-element.21), channel_id=1, source_target_pairs={{1,0},{2,1},{3,2},{0,3},{5,4},{6,5},{7,6},{4,7},{9,8},{10,9},{11,1... | collective-permute-start | bytes 1179656 | tf_op jit(solution)/shard_map/ppermute | solution.py:724
  5.3 1.7 %collective-permute-start.3 = (bf16[4,54,256]{2,1,0:T(8,128)(2,1)}, bf16[4,54,256]{2,1,0:T(8,128)(2,1)S(1)}, u32[]{:S(2)}, u32[]{:S(2)}) collective-permute-start(bf16[4,54,256]{2,1,0:T(8,128)(2,1)} %get-tuple-element.24), channel_id=1, source_target_pairs={{1,0},{2,1},{3,2},{0,3},{5,4},{6,5},{7,6},{4,7},{9,8},{10,9},{11,1... | collective-permute-start | bytes 331784 | tf_op jit(solution)/shard_map/ppermute | solution.py:722
  7.1 0.1 stack.27.place_ref
  7.1 8.0 %inner.1 = (f32[2,16,6,16,256]{4,3,2,1,0:T(8,128)S(1)}, f32[2,16,6,16,256]{4,3,2,1,0:T(8,128)S(1)}, f32[16,112,256]{2,1,0:T(8,128)S(1)}, f32[16,24,256]{2,1,0:T(8,128)S(1)}, f32[24,256]{1,0:T(8,128)S(1)}) custom-call(f32[6,512,128]{2,1,0:T(8,128)S(1)} %bitcast.24, f32[864,128]{1,0:T(8,128)S(1)} %bitcast.26), custom_call_target="tpu_custom_call" | custom-call | flops 1000000 | bytes 24000000 | tf_op jit(solution)/shard_map/inner/pallas_call | solution.py:431
  15.1 1.8 %collective-permute-done.2.lo_ref = bf16[4,54,256]{2,1,0:T(8,128)(2,1)S(1)} collective-permute-done((bf16[4,54,256]{2,1,0:T(8,128)(2,1)}, bf16[4,54,256]{2,1,0:T(8,128)(2,1)S(1)}, u32[]{:S(2)}, u32[]{:S(2)}) %collective-permute-start.2) | collective-permute-done | bytes 110624 | tf_op jit(solution)/shard_map/ppermute | solution.py:721
  16.9 1.2 %gauge_halo.1 = (f32[16,112,256]{2,1,0:T(8,128)S(1)}, f32[16,24,256]{2,1,0:T(8,128)S(1)}) custom-call(f32[24,256]{1,0:T(8,128)S(1)} %get-tuple-element.22.top_ref, bf16[4,54,256]{2,1,0:T(8,128)(2,1)S(1)} %collective-permute-done.2.lo_ref, bf16[4,54,256]{2,1,0:T(8,128)(2,1)S(1)} %collective-permute-done.3.hi_ref, ...), custom_call_target="tpu_custom_call" | custom-call | flops 1000000 | bytes 4500000 | tf_op jit(solution)/shard_map/gauge_halo/pallas_call | solution.py:288
  18.1 16.0 %outer.1 = (bf16[2,8,6,16,256]{4,3,2,1,0:T(8,128)(2,1)S(1)}, bf16[4,2,6,32,128]{4,3,2,1,0:T(8,128)(2,1)S(1)}, bf16[4,2,6,32,128]{4,3,2,1,0:T(8,128)(2,1)S(1)}) custom-call(s32[5]{0:T(128)S(1)} %stack.27.place_ref, bf16[4,2,6,16,256]{4,3,2,1,0:T(8,128)(2,1)S(1)} %collective-permute-done.lo_ref, bf16[4,2,6,16,256]{4,3,2,1,0:T(8,128)(2,1)S(1)} %collective-permute-done.1.hi_ref, ...), custom_call_target="tpu_custom_call" | custom-call | flops 1000000 | bytes 48000000 | tf_op jit(solution)/shard_map/outer/pallas_call | solution.py:514
  34.1 0.1 weights.1.weight_ref
  34.2 10.4 %correlate.1 = f32[4,64,112]{2,1,0:T(8,128)S(1)} custom-call(s32[5]{0:T(128)S(1)} %stack.27.place_ref, bf16[448,6,8,256]{3,2,1,0:T(8,128)(2,1)S(1)} %bitcast.22, bf16[512,1536]{1,0:T(8,128)(2,1)S(1)} %weights.1.weight_ref), custom_call_target="tpu_custom_call" | custom-call | flops 1000000 | bytes 33000000 | tf_op jit(solution)/shard_map/correlate/pallas_call | solution.py:589
  44.7 0.7 collective-permute-start.6
  45.3 0.1 collective-permute-start.4
  45.4 1.3 %collective-permute-done.4 = f32[2,64,112]{2,1,0:T(8,128)S(1)} collective-permute-done((f32[2,64,112]{2,1,0:T(8,128)S(1)}, f32[2,64,112]{2,1,0:T(8,128)S(1)}, u32[]{:S(2)}, u32[]{:S(2)}) %collective-permute-start.4) | collective-permute-done | bytes 57376 | tf_op jit(solution)/shard_map/ppermute | solution.py:750
  46.8 0.5 collective-permute-start.5
  47.3 0.2 order.1.order_ref
  47.6 3.1 %collective-permute-start.7 = (bf16[2,2,6,32,128]{4,3,2,1,0:T(8,128)(2,1)S(1)}, bf16[2,2,6,32,128]{4,3,2,1,0:T(8,128)(2,1)S(1)}, u32[]{:S(2)}, u32[]{:S(2)}) collective-permute-start(bf16[2,2,6,32,128]{4,3,2,1,0:T(8,128)(2,1)S(1)} %get-tuple-element.34), channel_id=1, source_target_pairs={{0,0},{1,4},{2,8},{3,12},{4,16},{5,20},{6,24},{7,28},{8,1},{9,5},{... | collective-permute-start | bytes 589832 | tf_op jit(solution)/shard_map/ppermute | solution.py:742
  50.7 4.2 %collective-permute-start.8 = (bf16[2,2,6,32,128]{4,3,2,1,0:T(8,128)(2,1)S(1)}, bf16[2,2,6,32,128]{4,3,2,1,0:T(8,128)(2,1)S(1)}, u32[]{:S(2)}, u32[]{:S(2)}) collective-permute-start(bf16[2,2,6,32,128]{4,3,2,1,0:T(8,128)(2,1)S(1)} %get-tuple-element.35), channel_id=1, source_target_pairs={{0,8},{1,12},{2,16},{3,20},{4,24},{5,28},{6,0},{7,4},{8,9},{9,13},... | collective-permute-start | bytes 589832 | tf_op jit(solution)/shard_map/ppermute | solution.py:742
  54.9 4.0 %collective-permute-start.9 = (bf16[2,2,6,32,128]{4,3,2,1,0:T(8,128)(2,1)S(1)}, bf16[2,2,6,32,128]{4,3,2,1,0:T(8,128)(2,1)S(1)}, u32[]{:S(2)}, u32[]{:S(2)}) collective-permute-start(bf16[2,2,6,32,128]{4,3,2,1,0:T(8,128)(2,1)S(1)} %get-tuple-element.36), channel_id=1, source_target_pairs={{0,16},{1,20},{2,24},{3,28},{4,0},{5,4},{6,8},{7,12},{8,17},{9,21}... | collective-permute-start | bytes 589832 | tf_op jit(solution)/shard_map/ppermute | solution.py:742
  58.9 1.9 %collective-permute-start.10 = (bf16[2,2,6,32,128]{4,3,2,1,0:T(8,128)(2,1)S(1)}, bf16[2,2,6,32,128]{4,3,2,1,0:T(8,128)(2,1)S(1)}, u32[]{:S(2)}, u32[]{:S(2)}) collective-permute-start(bf16[2,2,6,32,128]{4,3,2,1,0:T(8,128)(2,1)S(1)} %get-tuple-element.37), channel_id=1, source_target_pairs={{0,24},{1,28},{2,0},{3,4},{4,8},{5,12},{6,16},{7,20},{8,25},{9,29}... | collective-permute-start | bytes 589832 | tf_op jit(solution)/shard_map/ppermute | solution.py:742
  60.9 0.6 fusion.1
  61.5 9.4 %collective-permute-done.8.refs_1_ = bf16[2,2,6,32,128]{4,3,2,1,0:T(8,128)(2,1)S(1)} collective-permute-done((bf16[2,2,6,32,128]{4,3,2,1,0:T(8,128)(2,1)S(1)}, bf16[2,2,6,32,128]{4,3,2,1,0:T(8,128)(2,1)S(1)}, u32[]{:S(2)}, u32[]{:S(2)}) %collective-permute-start.8) | collective-permute-done | bytes 196640 | tf_op jit(solution)/shard_map/ppermute | solution.py:742
  70.9 2.9 %collective-permute-done.9.refs_2_ = bf16[2,2,6,32,128]{4,3,2,1,0:T(8,128)(2,1)S(1)} collective-permute-done((bf16[2,2,6,32,128]{4,3,2,1,0:T(8,128)(2,1)S(1)}, bf16[2,2,6,32,128]{4,3,2,1,0:T(8,128)(2,1)S(1)}, u32[]{:S(2)}, u32[]{:S(2)}) %collective-permute-start.9) | collective-permute-done | bytes 196640 | tf_op jit(solution)/shard_map/ppermute | solution.py:742
  73.7 3.5 %collective-permute-done.10.refs_3_ = bf16[2,2,6,32,128]{4,3,2,1,0:T(8,128)(2,1)S(1)} collective-permute-done((bf16[2,2,6,32,128]{4,3,2,1,0:T(8,128)(2,1)S(1)}, bf16[2,2,6,32,128]{4,3,2,1,0:T(8,128)(2,1)S(1)}, u32[]{:S(2)}, u32[]{:S(2)}) %collective-permute-start.10) | collective-permute-done | bytes 196640 | tf_op jit(solution)/shard_map/ppermute | solution.py:742
  77.2 3.3 %arrange.1 = bf16[2,32,32,192]{3,2,1,0:T(8,128)(2,1)} custom-call(s32[5]{0:T(128)S(1)} %stack.27.place_ref, bf16[512,512]{1,0:T(8,128)(2,1)S(1)} %order.1.order_ref, bf16[2,2,6,32,128]{4,3,2,1,0:T(8,128)(2,1)S(1)} %collective-permute-done.7.refs_0_, bf16[2,2,6,32,128]{4,3,2,1,0:T(8,128)(2,1)S(1)} %collective-permute-done.8.refs_1_, ...), custom_call_target="tpu_custom_call" | custom-call | flops 1000000 | bytes 9000000 | tf_op jit(solution)/shard_map/arrange/pallas_call | solution.py:686
  (18 shorter events, 0.2 us)
Async XLA Ops:
  0.6 6.5 %copy-start.1 = (f32[1,2,3,32,8,256]{5,4,3,2,1,0:T(8,128)S(1)}, f32[1,2,3,32,8,256]{5,4,3,2,1,0:T(8,128)}, u32[]{:S(2)}) copy-start(f32[1,2,3,32,8,256]{5,4,3,2,1,0:T(8,128)} %param.3) | copy-start | bytes 4718596
  0.6 6.5 %copy-start.2 = (f32[1,3,2,3,3,8,256]{6,5,4,3,2,1,0:T(8,128)S(1)}, f32[1,3,2,3,3,8,256]{6,5,4,3,2,1,0:T(8,128)}, u32[]{:S(2)}) copy-start(f32[1,3,2,3,3,8,256]{6,5,4,3,2,1,0:T(8,128)} %param.4) | copy-start | bytes 1327108
  3.5 14.5 %collective-permute-start = (bf16[4,2,6,16,256]{4,3,2,1,0:T(8,128)(2,1)}, bf16[4,2,6,16,256]{4,3,2,1,0:T(8,128)(2,1)S(1)}, u32[]{:S(2)}, u32[]{:S(2)}) collective-permute-start(bf16[4,2,6,16,256]{4,3,2,1,0:T(8,128)(2,1)} %get-tuple-element.20), channel_id=1, source_target_pairs={{0,1},{1,2},{2,3},{3,0},{4,5},{5,6},{6,7},{7,4},{8,9},{9,10},{10,1... | collective-permute-start | bytes 1179656 | tf_op jit(solution)/shard_map/ppermute | solution.py:723
  3.6 14.5 %collective-permute-start.1 = (bf16[4,2,6,16,256]{4,3,2,1,0:T(8,128)(2,1)}, bf16[4,2,6,16,256]{4,3,2,1,0:T(8,128)(2,1)S(1)}, u32[]{:S(2)}, u32[]{:S(2)}) collective-permute-start(bf16[4,2,6,16,256]{4,3,2,1,0:T(8,128)(2,1)} %get-tuple-element.21), channel_id=1, source_target_pairs={{1,0},{2,1},{3,2},{0,3},{5,4},{6,5},{7,6},{4,7},{9,8},{10,9},{11,1... | collective-permute-start | bytes 1179656 | tf_op jit(solution)/shard_map/ppermute | solution.py:724
  5.3 11.6 %collective-permute-start.2 = (bf16[4,54,256]{2,1,0:T(8,128)(2,1)}, bf16[4,54,256]{2,1,0:T(8,128)(2,1)S(1)}, u32[]{:S(2)}, u32[]{:S(2)}) collective-permute-start(bf16[4,54,256]{2,1,0:T(8,128)(2,1)} %get-tuple-element.23), channel_id=1, source_target_pairs={{0,1},{1,2},{2,3},{3,0},{4,5},{5,6},{6,7},{7,4},{8,9},{9,10},{10,1... | collective-permute-start | bytes 331784 | tf_op jit(solution)/shard_map/ppermute | solution.py:721
  5.3 11.6 %collective-permute-start.3 = (bf16[4,54,256]{2,1,0:T(8,128)(2,1)}, bf16[4,54,256]{2,1,0:T(8,128)(2,1)S(1)}, u32[]{:S(2)}, u32[]{:S(2)}) collective-permute-start(bf16[4,54,256]{2,1,0:T(8,128)(2,1)} %get-tuple-element.24), channel_id=1, source_target_pairs={{1,0},{2,1},{3,2},{0,3},{5,4},{6,5},{7,6},{4,7},{9,8},{10,9},{11,1... | collective-permute-start | bytes 331784 | tf_op jit(solution)/shard_map/ppermute | solution.py:722
  18.1 16.2 %copy-start = (bf16[1,448,2,3,8,256]{5,4,3,2,1,0:T(8,128)(2,1)S(1)}, bf16[1,448,2,3,8,256]{5,4,3,2,1,0:T(8,128)(2,1)}, u32[]{:S(2)}) copy-start(bf16[1,448,2,3,8,256]{5,4,3,2,1,0:T(8,128)(2,1)} %param.5) | copy-start | bytes 33030148
  44.7 2.9 %collective-permute-start.6 = (bf16[4,2,6,32,128]{4,3,2,1,0:T(8,128)(2,1)S(1)}, bf16[4,2,6,32,128]{4,3,2,1,0:T(8,128)(2,1)S(1)}, u32[]{:S(2)}, u32[]{:S(2)}) collective-permute-start(bf16[4,2,6,32,128]{4,3,2,1,0:T(8,128)(2,1)S(1)} %get-tuple-element.33), channel_id=1, source_target_pairs={{0,1},{1,0},{2,3},{3,2},{4,5},{5,4},{6,7},{7,6},{8,9},{9,8},{10,11... | collective-permute-start | bytes 1179656 | tf_op jit(solution)/shard_map/ppermute | solution.py:732
  45.3 1.4 %collective-permute-start.4 = (f32[2,64,112]{2,1,0:T(8,128)S(1)}, f32[2,64,112]{2,1,0:T(8,128)S(1)}, u32[]{:S(2)}, u32[]{:S(2)}) collective-permute-start(f32[2,64,112]{2,1,0:T(8,128)S(1)} %pad_maximum_fusion), channel_id=1, source_target_pairs={{0,1},{1,0},{2,3},{3,2},{4,5},{5,4},{6,7},{7,6},{8,9},{9,8},{10,11... | collective-permute-start | bytes 172040 | tf_op jit(solution)/shard_map/ppermute | solution.py:750
  46.8 14.1 %collective-permute-start.5 = (f32[1,64,112]{2,1,0:T(8,128)S(1)}, f32[1,64,112]{2,1,0:T(8,128)S(1)}, u32[]{:S(2)}, u32[]{:S(2)}) collective-permute-start(f32[1,64,112]{2,1,0:T(8,128)S(1)} %slice_add_fusion), channel_id=1, source_target_pairs={{0,2},{1,3},{2,0},{3,1},{4,6},{5,7},{6,4},{7,5},{8,10},{9,11},{10,... | collective-permute-start | bytes 86024 | tf_op jit(solution)/shard_map/ppermute | solution.py:750
  47.6 13.9 %collective-permute-start.7 = (bf16[2,2,6,32,128]{4,3,2,1,0:T(8,128)(2,1)S(1)}, bf16[2,2,6,32,128]{4,3,2,1,0:T(8,128)(2,1)S(1)}, u32[]{:S(2)}, u32[]{:S(2)}) collective-permute-start(bf16[2,2,6,32,128]{4,3,2,1,0:T(8,128)(2,1)S(1)} %get-tuple-element.34), channel_id=1, source_target_pairs={{0,0},{1,4},{2,8},{3,12},{4,16},{5,20},{6,24},{7,28},{8,1},{9,5},{... | collective-permute-start | bytes 589832 | tf_op jit(solution)/shard_map/ppermute | solution.py:742
  50.7 20.1 %collective-permute-start.8 = (bf16[2,2,6,32,128]{4,3,2,1,0:T(8,128)(2,1)S(1)}, bf16[2,2,6,32,128]{4,3,2,1,0:T(8,128)(2,1)S(1)}, u32[]{:S(2)}, u32[]{:S(2)}) collective-permute-start(bf16[2,2,6,32,128]{4,3,2,1,0:T(8,128)(2,1)S(1)} %get-tuple-element.35), channel_id=1, source_target_pairs={{0,8},{1,12},{2,16},{3,20},{4,24},{5,28},{6,0},{7,4},{8,9},{9,13},... | collective-permute-start | bytes 589832 | tf_op jit(solution)/shard_map/ppermute | solution.py:742
  54.9 18.8 %collective-permute-start.9 = (bf16[2,2,6,32,128]{4,3,2,1,0:T(8,128)(2,1)S(1)}, bf16[2,2,6,32,128]{4,3,2,1,0:T(8,128)(2,1)S(1)}, u32[]{:S(2)}, u32[]{:S(2)}) collective-permute-start(bf16[2,2,6,32,128]{4,3,2,1,0:T(8,128)(2,1)S(1)} %get-tuple-element.36), channel_id=1, source_target_pairs={{0,16},{1,20},{2,24},{3,28},{4,0},{5,4},{6,8},{7,12},{8,17},{9,21}... | collective-permute-start | bytes 589832 | tf_op jit(solution)/shard_map/ppermute | solution.py:742
  58.9 18.3 %collective-permute-start.10 = (bf16[2,2,6,32,128]{4,3,2,1,0:T(8,128)(2,1)S(1)}, bf16[2,2,6,32,128]{4,3,2,1,0:T(8,128)(2,1)S(1)}, u32[]{:S(2)}, u32[]{:S(2)}) collective-permute-start(bf16[2,2,6,32,128]{4,3,2,1,0:T(8,128)(2,1)S(1)} %get-tuple-element.37), channel_id=1, source_target_pairs={{0,24},{1,28},{2,0},{3,4},{4,8},{5,12},{6,16},{7,20},{8,25},{9,29}... | collective-permute-start | bytes 589832 | tf_op jit(solution)/shard_map/ppermute | solution.py:742
where the time goes:
time: 80.7 us; the launch traced here: 80.5 us
  Pallas kernels  42.1 us (52%)
  waiting for transfers between devices  18.9 us (23%)
  starting transfers between devices  18 us (22%)
    pallas_call x1, Pallas kernels, run_outer(): pl.pallas_call(functools.partial(outer_kernel, layers=layers, parts=parts...  16 us
    ppermute x4, waiting for transfers between devices, shards(): sent.append(lax.ppermute(block, ('tm', 'space'), table_of))  15.8 us
    ppermute x4, starting transfers between devices, shards(): sent.append(lax.ppermute(block, ('tm', 'space'), table_of))  13.2 us
    pallas_call x1, Pallas kernels, run_corr(): pl.pallas_call(functools.partial(corr_kernel, layers=layers), grid_spec=g...  10.4 us
    pallas_call x1, Pallas kernels, run_inner(): pl.pallas_call(functools.partial(inner_kernel, layers=layers), in_specs=[...  7.96 us
    pallas_call x1, Pallas kernels, run_arrange(): pl.pallas_call(functools.partial(arrange_kernel, layers=layers), grid_spe...  3.26 us
    pallas_call x1, Pallas kernels, run_pack(): pl.pallas_call(functools.partial(pack_kernel, layers=layers, tiles=tiles)...  2.85 us
    ppermute x1, waiting for transfers between devices, shards(): lo_links = lax.ppermute(up_links, 'space', up)  1.75 us
  transfers between devices with their start and end apart: 11, of which 5 were waited for; matrix products, arithmetic and copies ran while one was open for 1% of the time, Pallas kernels for 12%

commit v1 on v0

--- a/solution.py
+++ b/solution.py
@@ -491,18 +491,17 @@
 
     lax.fori_loop(0, groups * (layers // 2), last, 0)
 
-    me, shift = place_ref[0], place_ref[1]
+    side, base = place_ref[0], place_ref[1]
     pairs = parts // 2
     width = planes // parts
     for g in range(groups):
         for k in range(6):
             turned = jnp.concatenate([pack_ref[g, k, :, cols(t)].T for t in range(tiles)], axis=0)
             for m in range(pairs):
-                even = turned[2 * m * width : (2 * m + 1) * width].astype(jnp.bfloat16)
-                odd = turned[(2 * m + 1) * width : (2 * m + 2) * width].astype(jnp.bfloat16)
-                at = lax.rem(m - shift + pairs, pairs)
-                keep_ref[at, g, k] = jnp.where(me == 0, even, odd)
-                give_ref[at, g, k] = jnp.where(me == 0, odd, even)
+                near = turned[m * width : (m + 1) * width].astype(jnp.bfloat16)
+                far = turned[(pairs + m) * width : (pairs + m + 1) * width].astype(jnp.bfloat16)
+                keep_ref[base ^ m, g, k] = jnp.where(side == 0, near, far)
+                give_ref[base ^ m, g, k] = jnp.where(side == 0, far, near)
 
 
 def run_outer(place, lo, hi, table, gauge, a, b, layers, parts):
@@ -639,53 +638,40 @@
     )()
 
 
-def arrange_kernel(place_ref, order_ref, *refs, layers):
+def arrange_kernel(place_ref, order_ref, *refs, layers, per):
     out_ref = refs[-1]
     groups, comps, width = refs[0].shape[1:4]
     span = 2 * groups * VB
-    side = place_ref[4]
-
-    def move(block_ref):
+    pieces = []
+    for ref in refs[:-1]:
         for h in range(2):
-            core = side if h == 0 else 1 - side
-            pieces = []
             for pair in range(comps // 2):
-                lanes = [
-                    block_ref[h, g, 2 * pair + bit] for bit in range(2) for g in range(groups)
-                ]
+                lanes = [ref[h, g, 2 * pair + bit] for bit in range(2) for g in range(groups)]
                 pieces.append(jnp.concatenate(lanes, axis=1))
-            moved = jnp.dot(
-                jnp.concatenate(pieces, axis=0), order_ref[...], preferred_element_type=jnp.float32
-            )
+    moved = jnp.dot(
+        jnp.concatenate(pieces, axis=0), order_ref[...], preferred_element_type=jnp.float32
+    )
+    for step in range(len(refs) - 1):
+        source = place_ref[3] ^ step
+        slice_at, chip = lax.rem(source, per), source // per
+        for h in range(2):
+            first = (2 * chip + (place_ref[4] ^ h)) * layers
+            at = (2 * step + h) * (comps // 2) * width
             for x in range(layers):
-                out_ref[core * layers + x] = jnp.concatenate(
+                out_ref[slice_at, first + x] = jnp.concatenate(
                     [
-                        moved[p * width : (p + 1) * width, x * span : (x + 1) * span]
+                        moved[at + p * width : at + (p + 1) * width, x * span : (x + 1) * span]
                         for p in range(comps // 2)
                     ],
                     axis=1,
                 ).astype(jnp.bfloat16)
 
-    for step, ref in enumerate(refs[:-1]):
-        pl.when(pl.program_id(0) == step)(functools.partial(move, ref))
-
-
-def run_arrange(place, order, blocks, shape, layers, near):
-    pairs = len(blocks)
-
-    def where(g, s):
-        source = lax.rem(s[3] - g + pairs, pairs)
-        return source // near, lax.rem(source, near), 0, 0
-
-    grid_spec = pltpu.PrefetchScalarGridSpec(
-        num_scalar_prefetch=1,
-        grid=(pairs,),
-        in_specs=in_vmem(1 + pairs),
-        out_specs=pl.BlockSpec((pl.Squeezed(), 2 * layers) + shape[2:], where),
-    )
-    return pl.pallas_call(
-        functools.partial(arrange_kernel, layers=layers),
-        grid_spec=grid_spec,
+
+def run_arrange(place, order, blocks, shape, layers, per):
+    return pl.pallas_call(
+        functools.partial(arrange_kernel, layers=layers, per=per),
+        in_specs=[in_smem()] + in_vmem(1 + len(blocks)),
+        out_specs=in_vmem(1)[0],
         out_shape=jax.ShapeDtypeStruct(shape, jnp.bfloat16),
         compiler_params=params(),
         cost_estimate=cost(3),
@@ -698,12 +684,20 @@
     comps = parts * colours
     tm, space = lax.axis_index("tm"), lax.axis_index("space")
     per = n_tm // n_space
-    near = n_space // 2
     pairs = n_tm // 2
     groups = vectors // VB
-    core = lax.rem(space, 2)
+
+    def base_of(i, j):
+        return (j // 2 * per + i % per) ^ (i // per % 2 * per)
+
     place = jnp.stack(
-        [core, lax.rem(tm, per) * near + space // 2, space, tm // 2, lax.rem(tm, 2)]
+        [
+            space % 2 ^ tm // pairs,
+            base_of(tm, space),
+            space,
+            tm % pairs ^ space % 2 * per,
+            tm // pairs ^ space * per // pairs,
+        ]
     ).astype(jnp.int32)
 
     tiles = planes // LANES
@@ -732,15 +726,17 @@
     got = lax.ppermute(give, "space", [(i, i ^ 1) for i in range(n_space)])
     blocks = run_merge(keep, got)
     stored = stored_vectors.reshape(stored_vectors.shape[1], comps, layers, planes)
-    sent = []
-    for step, block in enumerate(blocks):
+    sent = [None] * pairs
+    digits = pairs.bit_length() - 1
+    for step in sorted(range(pairs), key=lambda n: f"{n:0{digits}b}"[::-1]):
         table_of = []
         for i in range(n_tm):
             for j in range(n_space):
-                m = ((i % per) * near + j // 2 + step) % pairs
-                table_of.append((i * n_space + j, (2 * m + j % 2) * n_space + i // per))
-        sent.append(lax.ppermute(block, ("tm", "space"), table_of))
+                to = (j % 2 ^ i // pairs) * pairs + (base_of(i, j) ^ step)
+                table_of.append((i * n_space + j, to * n_space + i // per))
+        sent[step] = lax.ppermute(blocks[step], ("tm", "space"), table_of)
     partial = run_corr(place, stored, weights, n_space)
+    partial, *sent = lax.optimization_barrier((partial, *sent))
     sums = {d: partial[d] for d in range(n_space)}
 
     bit = 1
@@ -755,7 +751,7 @@
     correlations = sums[0].T[None]
 
     shape = (per, n_space * layers, planes // n_tm, comps * vectors)
-    return correlations, run_arrange(place, order, sent, shape, layers, near)
+    return correlations, run_arrange(place, order, sent, shape, layers, per)
 
 
 def solution(mesh):

time: 80.7 us -> 67.3 us (0.83)
  the two profiles are of different devices: /device:TPU:12 before, /device:TPU:0 now
where the time goes in v1:
time: 67.3 us; the launch traced here: 67.2 us
  Pallas kernels  40.9 us (61%)
  starting transfers between devices  19.7 us (29%)
  waiting for transfers between devices  5 us (7%)
  between operations  0.8 us (1%)
    pallas_call x1, Pallas kernels, run_outer(): pl.pallas_call(functools.partial(outer_kernel, layers=layers, parts=parts...  16 us
    ppermute x4, starting transfers between devices, shards(): sent[step] = lax.ppermute(blocks[step], ('tm', 'space'), table_of)  11 us
    pallas_call x1, Pallas kernels, run_corr(): pl.pallas_call(functools.partial(corr_kernel, layers=layers), grid_spec=g...  10.4 us
    pallas_call x1, Pallas kernels, run_inner(): pl.pallas_call(functools.partial(inner_kernel, layers=layers), in_specs=[...  7.96 us
    ppermute x2, starting transfers between devices, shards(): came = lax.ppermute(jnp.stack([sums[d] for d in going]), 'space', partner)  4.32 us
    pallas_call x1, Pallas kernels, run_pack(): pl.pallas_call(functools.partial(pack_kernel, layers=layers, tiles=tiles)...  2.85 us
    ppermute x1, waiting for transfers between devices, shards(): hi_links = lax.ppermute(down_links, 'space', down)  2.38 us
    pallas_call x1, Pallas kernels, run_arrange(): pl.pallas_call(functools.partial(arrange_kernel, layers=layers, per=per),...  2.16 us
  transfers between devices with their start and end apart: 11, of which 3 were waited for; matrix products, arithmetic and copies ran while one was open for 0% of the time, Pallas kernels for 33%

profile of v1, /device:TPU:0, one launch (start us, length us, event | category | flops | bytes accessed | tf_op | source)
XLA Modules:
  0.0 67.2 jit_solution(6488421412975151045)
XLA Ops:
  0.6 2.8 %pack.1 = (bf16[4,54,256]{2,1,0:T(8,128)(2,1)}, bf16[4,54,256]{2,1,0:T(8,128)(2,1)}, bf16[4,2,6,16,256]{4,3,2,1,0:T(8,128)(2,1)}, bf16[4,2,6,16,256]{4,3,2,1,0:T(8,128)(2,1)}) custom-call(f32[6,512,128]{2,1,0:T(8,128)} %bitcast.23, f32[864,128]{1,0:T(8,128)} %bitcast.25), custom_call_target="tpu_custom_call" | custom-call | flops 1000000 | bytes 7500000 | tf_op jit(solution)/shard_map/pack/pallas_call | solution.py:98
  3.5 0.5 collective-permute-start
  4.0 2.0 %collective-permute-start.1 = (bf16[4,2,6,16,256]{4,3,2,1,0:T(8,128)(2,1)}, bf16[4,2,6,16,256]{4,3,2,1,0:T(8,128)(2,1)S(1)}, u32[]{:S(2)}, u32[]{:S(2)}) collective-permute-start(bf16[4,2,6,16,256]{4,3,2,1,0:T(8,128)(2,1)} %get-tuple-element.26), channel_id=1, source_target_pairs={{1,0},{2,1},{3,2},{0,3},{5,4},{6,5},{7,6},{4,7},{9,8},{10,9},{11,1... | collective-permute-start | bytes 1179656 | tf_op jit(solution)/shard_map/ppermute | solution.py:718
  6.0 0.6 collective-permute-start.2
  6.6 1.1 %collective-permute-start.3 = (bf16[4,54,256]{2,1,0:T(8,128)(2,1)}, bf16[4,54,256]{2,1,0:T(8,128)(2,1)S(1)}, u32[]{:S(2)}, u32[]{:S(2)}) collective-permute-start(bf16[4,54,256]{2,1,0:T(8,128)(2,1)} %get-tuple-element.29), channel_id=1, source_target_pairs={{1,0},{2,1},{3,2},{0,3},{5,4},{6,5},{7,6},{4,7},{9,8},{10,9},{11,1... | collective-permute-start | bytes 331784 | tf_op jit(solution)/shard_map/ppermute | solution.py:716
  7.8 0.1 stack.27.place_ref
  7.9 8.0 %inner.1 = (f32[2,16,6,16,256]{4,3,2,1,0:T(8,128)S(1)}, f32[2,16,6,16,256]{4,3,2,1,0:T(8,128)S(1)}, f32[16,112,256]{2,1,0:T(8,128)S(1)}, f32[16,24,256]{2,1,0:T(8,128)S(1)}, f32[24,256]{1,0:T(8,128)S(1)}) custom-call(f32[6,512,128]{2,1,0:T(8,128)S(1)} %bitcast.24, f32[864,128]{1,0:T(8,128)S(1)} %bitcast.26), custom_call_target="tpu_custom_call" | custom-call | flops 1000000 | bytes 24000000 | tf_op jit(solution)/shard_map/inner/pallas_call | solution.py:431
  15.8 2.4 %collective-permute-done.3.hi_ref = bf16[4,54,256]{2,1,0:T(8,128)(2,1)S(1)} collective-permute-done((bf16[4,54,256]{2,1,0:T(8,128)(2,1)}, bf16[4,54,256]{2,1,0:T(8,128)(2,1)S(1)}, u32[]{:S(2)}, u32[]{:S(2)}) %collective-permute-start.3) | collective-permute-done | bytes 110624 | tf_op jit(solution)/shard_map/ppermute | solution.py:716
  18.2 1.2 %gauge_halo.1 = (f32[16,112,256]{2,1,0:T(8,128)S(1)}, f32[16,24,256]{2,1,0:T(8,128)S(1)}) custom-call(f32[24,256]{1,0:T(8,128)S(1)} %get-tuple-element.27.top_ref, bf16[4,54,256]{2,1,0:T(8,128)(2,1)S(1)} %collective-permute-done.2.lo_ref, bf16[4,54,256]{2,1,0:T(8,128)(2,1)S(1)} %collective-permute-done.3.hi_ref, ...), custom_call_target="tpu_custom_call" | custom-call | flops 1000000 | bytes 4500000 | tf_op jit(solution)/shard_map/gauge_halo/pallas_call | solution.py:288
  19.4 16.0 %outer.1 = (bf16[2,8,6,16,256]{4,3,2,1,0:T(8,128)(2,1)S(1)}, bf16[4,2,6,32,128]{4,3,2,1,0:T(8,128)(2,1)S(1)}, bf16[4,2,6,32,128]{4,3,2,1,0:T(8,128)(2,1)S(1)}) custom-call(s32[5]{0:T(128)S(1)} %stack.27.place_ref, bf16[4,2,6,16,256]{4,3,2,1,0:T(8,128)(2,1)S(1)} %collective-permute-done.lo_ref, bf16[4,2,6,16,256]{4,3,2,1,0:T(8,128)(2,1)S(1)} %collective-permute-done.1.hi_ref, ...), custom_call_target="tpu_custom_call" | custom-call | flops 1000000 | bytes 48000000 | tf_op jit(solution)/shard_map/outer/pallas_call | solution.py:513
  35.4 0.1 collective-permute-start.4
  35.5 1.7 %collective-permute-done.4.got_ref = bf16[4,2,6,32,128]{4,3,2,1,0:T(8,128)(2,1)S(1)} collective-permute-done((bf16[4,2,6,32,128]{4,3,2,1,0:T(8,128)(2,1)S(1)}, bf16[4,2,6,32,128]{4,3,2,1,0:T(8,128)(2,1)S(1)}, u32[]{:S(2)}, u32[]{:S(2)}) %collective-permute-start.4) | collective-permute-done | bytes 393248 | tf_op jit(solution)/shard_map/ppermute | solution.py:726
  37.3 0.7 %collective-permute-start.5 = (bf16[2,2,6,32,128]{4,3,2,1,0:T(8,128)(2,1)S(1)}, bf16[2,2,6,32,128]{4,3,2,1,0:T(8,128)(2,1)S(1)}, u32[]{:S(2)}, u32[]{:S(2)}) collective-permute-start(bf16[2,2,6,32,128]{4,3,2,1,0:T(8,128)(2,1)S(1)} %get-tuple-element.39), channel_id=1, source_target_pairs={{0,0},{1,16},{2,8},{3,24},{4,4},{5,20},{6,12},{7,28},{8,9},{9,25},... | collective-permute-start | bytes 589832 | tf_op jit(solution)/shard_map/ppermute | solution.py:737
  38.0 1.9 %collective-permute-start.6 = (bf16[2,2,6,32,128]{4,3,2,1,0:T(8,128)(2,1)S(1)}, bf16[2,2,6,32,128]{4,3,2,1,0:T(8,128)(2,1)S(1)}, u32[]{:S(2)}, u32[]{:S(2)}) collective-permute-start(bf16[2,2,6,32,128]{4,3,2,1,0:T(8,128)(2,1)S(1)} %get-tuple-element.40), channel_id=1, source_target_pairs={{0,4},{1,20},{2,12},{3,28},{4,0},{5,16},{6,8},{7,24},{8,13},{9,29}... | collective-permute-start | bytes 589832 | tf_op jit(solution)/shard_map/ppermute | solution.py:737
  39.8 7.0 %collective-permute-start.7 = (bf16[2,2,6,32,128]{4,3,2,1,0:T(8,128)(2,1)S(1)}, bf16[2,2,6,32,128]{4,3,2,1,0:T(8,128)(2,1)S(1)}, u32[]{:S(2)}, u32[]{:S(2)}) collective-permute-start(bf16[2,2,6,32,128]{4,3,2,1,0:T(8,128)(2,1)S(1)} %get-tuple-element.41), channel_id=1, source_target_pairs={{0,8},{1,24},{2,0},{3,16},{4,12},{5,28},{6,4},{7,20},{8,1},{9,17},... | collective-permute-start | bytes 589832 | tf_op jit(solution)/shard_map/ppermute | solution.py:737
  46.8 1.5 %collective-permute-start.8 = (bf16[2,2,6,32,128]{4,3,2,1,0:T(8,128)(2,1)S(1)}, bf16[2,2,6,32,128]{4,3,2,1,0:T(8,128)(2,1)S(1)}, u32[]{:S(2)}, u32[]{:S(2)}) collective-permute-start(bf16[2,2,6,32,128]{4,3,2,1,0:T(8,128)(2,1)S(1)} %get-tuple-element.42), channel_id=1, source_target_pairs={{0,12},{1,28},{2,4},{3,20},{4,8},{5,24},{6,0},{7,16},{8,5},{9,21},... | collective-permute-start | bytes 589832 | tf_op jit(solution)/shard_map/ppermute | solution.py:737
  48.3 0.1 weights.1.weight_ref
  48.4 10.4 %correlate.1 = f32[4,64,112]{2,1,0:T(8,128)S(1)} custom-call(s32[5]{0:T(128)S(1)} %stack.27.place_ref, bf16[448,6,8,256]{3,2,1,0:T(8,128)(2,1)S(1)} %bitcast.22, bf16[512,1536]{1,0:T(8,128)(2,1)S(1)} %weights.1.weight_ref), custom_call_target="tpu_custom_call" | custom-call | flops 1000000 | bytes 33000000 | tf_op jit(solution)/shard_map/correlate/pallas_call | solution.py:588
  58.9 2.1 %collective-permute-start.9 = (f32[2,64,112]{2,1,0:T(8,128)S(1)}, f32[2,64,112]{2,1,0:T(8,128)S(1)}, u32[]{:S(2)}, u32[]{:S(2)}) collective-permute-start(f32[2,64,112]{2,1,0:T(8,128)S(1)} %pad_maximum_fusion), channel_id=1, source_target_pairs={{0,1},{1,0},{2,3},{3,2},{4,5},{5,4},{6,7},{7,6},{8,9},{9,8},{10,11... | collective-permute-start | bytes 172040 | tf_op jit(solution)/shard_map/ppermute | solution.py:746
  61.0 0.9 %collective-permute-done.9 = f32[2,64,112]{2,1,0:T(8,128)S(1)} collective-permute-done((f32[2,64,112]{2,1,0:T(8,128)S(1)}, f32[2,64,112]{2,1,0:T(8,128)S(1)}, u32[]{:S(2)}, u32[]{:S(2)}) %collective-permute-start.9) | collective-permute-done | bytes 57376 | tf_op jit(solution)/shard_map/ppermute | solution.py:746
  61.9 2.2 %collective-permute-start.10 = (f32[1,64,112]{2,1,0:T(8,128)S(1)}, f32[1,64,112]{2,1,0:T(8,128)S(1)}, u32[]{:S(2)}, u32[]{:S(2)}) collective-permute-start(f32[1,64,112]{2,1,0:T(8,128)S(1)} %slice_add_fusion), channel_id=1, source_target_pairs={{0,2},{1,3},{2,0},{3,1},{4,6},{5,7},{6,4},{7,5},{8,10},{9,11},{10,... | collective-permute-start | bytes 86024 | tf_op jit(solution)/shard_map/ppermute | solution.py:746
  64.1 0.2 order.1.order_ref
  64.4 2.2 %arrange.1 = bf16[2,32,32,192]{3,2,1,0:T(8,128)(2,1)} custom-call(s32[5]{0:T(128)S(1)} %stack.27.place_ref, bf16[512,512]{1,0:T(8,128)(2,1)S(1)} %order.1.order_ref, bf16[2,2,6,32,128]{4,3,2,1,0:T(8,128)(2,1)S(1)} %collective-permute-done.5.refs_0_, bf16[2,2,6,32,128]{4,3,2,1,0:T(8,128)(2,1)S(1)} %collective-permute-done.6.refs_1_, ...), custom_call_target="tpu_custom_call" | custom-call | flops 1000000 | bytes 9000000 | tf_op jit(solution)/shard_map/arrange/pallas_call | solution.py:671
  66.5 0.6 fusion.1
  (18 shorter events, 0.1 us)
Async XLA Ops:
  0.6 7.2 %copy-start.1 = (f32[1,2,3,32,8,256]{5,4,3,2,1,0:T(8,128)S(1)}, f32[1,2,3,32,8,256]{5,4,3,2,1,0:T(8,128)}, u32[]{:S(2)}) copy-start(f32[1,2,3,32,8,256]{5,4,3,2,1,0:T(8,128)} %param.3) | copy-start | bytes 4718596
  0.6 7.2 %copy-start.2 = (f32[1,3,2,3,3,8,256]{6,5,4,3,2,1,0:T(8,128)S(1)}, f32[1,3,2,3,3,8,256]{6,5,4,3,2,1,0:T(8,128)}, u32[]{:S(2)}) copy-start(f32[1,3,2,3,3,8,256]{6,5,4,3,2,1,0:T(8,128)} %param.4) | copy-start | bytes 1327108
  3.5 15.9 %collective-permute-start = (bf16[4,2,6,16,256]{4,3,2,1,0:T(8,128)(2,1)}, bf16[4,2,6,16,256]{4,3,2,1,0:T(8,128)(2,1)S(1)}, u32[]{:S(2)}, u32[]{:S(2)}) collective-permute-start(bf16[4,2,6,16,256]{4,3,2,1,0:T(8,128)(2,1)} %get-tuple-element.25), channel_id=1, source_target_pairs={{0,1},{1,2},{2,3},{3,0},{4,5},{5,6},{6,7},{7,4},{8,9},{9,10},{10,1... | collective-permute-start | bytes 1179656 | tf_op jit(solution)/shard_map/ppermute | solution.py:717
  4.0 15.4 %collective-permute-start.1 = (bf16[4,2,6,16,256]{4,3,2,1,0:T(8,128)(2,1)}, bf16[4,2,6,16,256]{4,3,2,1,0:T(8,128)(2,1)S(1)}, u32[]{:S(2)}, u32[]{:S(2)}) collective-permute-start(bf16[4,2,6,16,256]{4,3,2,1,0:T(8,128)(2,1)} %get-tuple-element.26), channel_id=1, source_target_pairs={{1,0},{2,1},{3,2},{0,3},{5,4},{6,5},{7,6},{4,7},{9,8},{10,9},{11,1... | collective-permute-start | bytes 1179656 | tf_op jit(solution)/shard_map/ppermute | solution.py:718
  6.0 9.8 %collective-permute-start.2 = (bf16[4,54,256]{2,1,0:T(8,128)(2,1)}, bf16[4,54,256]{2,1,0:T(8,128)(2,1)S(1)}, u32[]{:S(2)}, u32[]{:S(2)}) collective-permute-start(bf16[4,54,256]{2,1,0:T(8,128)(2,1)} %get-tuple-element.28), channel_id=1, source_target_pairs={{0,1},{1,2},{2,3},{3,0},{4,5},{5,6},{6,7},{7,4},{8,9},{9,10},{10,1... | collective-permute-start | bytes 331784 | tf_op jit(solution)/shard_map/ppermute | solution.py:715
  6.6 11.6 %collective-permute-start.3 = (bf16[4,54,256]{2,1,0:T(8,128)(2,1)}, bf16[4,54,256]{2,1,0:T(8,128)(2,1)S(1)}, u32[]{:S(2)}, u32[]{:S(2)}) collective-permute-start(bf16[4,54,256]{2,1,0:T(8,128)(2,1)} %get-tuple-element.29), channel_id=1, source_target_pairs={{1,0},{2,1},{3,2},{0,3},{5,4},{6,5},{7,6},{4,7},{9,8},{10,9},{11,1... | collective-permute-start | bytes 331784 | tf_op jit(solution)/shard_map/ppermute | solution.py:716
  19.4 28.9 %copy-start = (bf16[1,448,2,3,8,256]{5,4,3,2,1,0:T(8,128)(2,1)S(1)}, bf16[1,448,2,3,8,256]{5,4,3,2,1,0:T(8,128)(2,1)}, u32[]{:S(2)}) copy-start(bf16[1,448,2,3,8,256]{5,4,3,2,1,0:T(8,128)(2,1)} %param.5) | copy-start | bytes 33030148
  35.4 1.8 %collective-permute-start.4 = (bf16[4,2,6,32,128]{4,3,2,1,0:T(8,128)(2,1)S(1)}, bf16[4,2,6,32,128]{4,3,2,1,0:T(8,128)(2,1)S(1)}, u32[]{:S(2)}, u32[]{:S(2)}) collective-permute-start(bf16[4,2,6,32,128]{4,3,2,1,0:T(8,128)(2,1)S(1)} %get-tuple-element.38), channel_id=1, source_target_pairs={{0,1},{1,0},{2,3},{3,2},{4,5},{5,4},{6,7},{7,6},{8,9},{9,8},{10,11... | collective-permute-start | bytes 1179656 | tf_op jit(solution)/shard_map/ppermute | solution.py:726
  37.3 21.5 %collective-permute-start.5 = (bf16[2,2,6,32,128]{4,3,2,1,0:T(8,128)(2,1)S(1)}, bf16[2,2,6,32,128]{4,3,2,1,0:T(8,128)(2,1)S(1)}, u32[]{:S(2)}, u32[]{:S(2)}) collective-permute-start(bf16[2,2,6,32,128]{4,3,2,1,0:T(8,128)(2,1)S(1)} %get-tuple-element.39), channel_id=1, source_target_pairs={{0,0},{1,16},{2,8},{3,24},{4,4},{5,20},{6,12},{7,28},{8,9},{9,25},... | collective-permute-start | bytes 589832 | tf_op jit(solution)/shard_map/ppermute | solution.py:737
  38.0 20.9 %collective-permute-start.6 = (bf16[2,2,6,32,128]{4,3,2,1,0:T(8,128)(2,1)S(1)}, bf16[2,2,6,32,128]{4,3,2,1,0:T(8,128)(2,1)S(1)}, u32[]{:S(2)}, u32[]{:S(2)}) collective-permute-start(bf16[2,2,6,32,128]{4,3,2,1,0:T(8,128)(2,1)S(1)} %get-tuple-element.40), channel_id=1, source_target_pairs={{0,4},{1,20},{2,12},{3,28},{4,0},{5,16},{6,8},{7,24},{8,13},{9,29}... | collective-permute-start | bytes 589832 | tf_op jit(solution)/shard_map/ppermute | solution.py:737
  39.8 19.0 %collective-permute-start.7 = (bf16[2,2,6,32,128]{4,3,2,1,0:T(8,128)(2,1)S(1)}, bf16[2,2,6,32,128]{4,3,2,1,0:T(8,128)(2,1)S(1)}, u32[]{:S(2)}, u32[]{:S(2)}) collective-permute-start(bf16[2,2,6,32,128]{4,3,2,1,0:T(8,128)(2,1)S(1)} %get-tuple-element.41), channel_id=1, source_target_pairs={{0,8},{1,24},{2,0},{3,16},{4,12},{5,28},{6,4},{7,20},{8,1},{9,17},... | collective-permute-start | bytes 589832 | tf_op jit(solution)/shard_map/ppermute | solution.py:737
  46.8 12.0 %collective-permute-start.8 = (bf16[2,2,6,32,128]{4,3,2,1,0:T(8,128)(2,1)S(1)}, bf16[2,2,6,32,128]{4,3,2,1,0:T(8,128)(2,1)S(1)}, u32[]{:S(2)}, u32[]{:S(2)}) collective-permute-start(bf16[2,2,6,32,128]{4,3,2,1,0:T(8,128)(2,1)S(1)} %get-tuple-element.42), channel_id=1, source_target_pairs={{0,12},{1,28},{2,4},{3,20},{4,8},{5,24},{6,0},{7,16},{8,5},{9,21},... | collective-permute-start | bytes 589832 | tf_op jit(solution)/shard_map/ppermute | solution.py:737
  58.9 3.0 %collective-permute-start.9 = (f32[2,64,112]{2,1,0:T(8,128)S(1)}, f32[2,64,112]{2,1,0:T(8,128)S(1)}, u32[]{:S(2)}, u32[]{:S(2)}) collective-permute-start(f32[2,64,112]{2,1,0:T(8,128)S(1)} %pad_maximum_fusion), channel_id=1, source_target_pairs={{0,1},{1,0},{2,3},{3,2},{4,5},{5,4},{6,7},{7,6},{8,9},{9,8},{10,11... | collective-permute-start | bytes 172040 | tf_op jit(solution)/shard_map/ppermute | solution.py:746
  61.9 4.6 %collective-permute-start.10 = (f32[1,64,112]{2,1,0:T(8,128)S(1)}, f32[1,64,112]{2,1,0:T(8,128)S(1)}, u32[]{:S(2)}, u32[]{:S(2)}) collective-permute-start(f32[1,64,112]{2,1,0:T(8,128)S(1)} %slice_add_fusion), channel_id=1, source_target_pairs={{0,2},{1,3},{2,0},{3,1},{4,6},{5,7},{6,4},{7,5},{8,10},{9,11},{10,... | collective-permute-start | bytes 86024 | tf_op jit(solution)/shard_map/ppermute | solution.py:746

commit v2 on v1

--- a/solution.py
+++ b/solution.py
@@ -562,14 +562,25 @@
     rows = jnp.concatenate(
         [stored_ref[:, k].reshape(block * layers, planes) for k in range(comps)], axis=1
     )
-    full = lax.dot_general(
-        rows, weight_ref[...], (((1,), (1,)), ((), ())), preferred_element_type=jnp.float32
-    )
-    layer_of_row = lax.broadcasted_iota(jnp.int32, (block * layers, span), 0) % layers
-    kept = jnp.zeros((block * layers, span), jnp.float32)
-    for x in range(layers):
-        kept = jnp.where(layer_of_row == x, full[:, x * span : (x + 1) * span], kept)
-    out_ref[...] = jnp.sum(kept.reshape(block, layers, span), axis=1).T
+    layer_of_row = lax.broadcasted_iota(jnp.int32, (block * layers, LANES), 0) % layers
+    layer_of_lane = lax.broadcasted_iota(jnp.int32, (block * layers, LANES), 1) // span
+    kept = jnp.zeros((block * layers, LANES), jnp.float32)
+    width = min(2 * LANES, weight_ref.shape[0])
+    for first in range(0, weight_ref.shape[0], width):
+        full = lax.dot_general(
+            rows,
+            weight_ref[first : first + width, :],
+            (((1,), (1,)), ((), ())),
+            preferred_element_type=jnp.float32,
+        )
+        for at in range(0, width, LANES):
+            here = layer_of_row == (first + at) // span + layer_of_lane
+            kept = jnp.where(here, full[:, at : at + LANES], kept)
+    summed = jnp.sum(kept.reshape(block, layers, LANES), axis=1)
+    total = summed[:, :span]
+    for at in range(span, LANES, span):
+        total = total + summed[:, at : at + span]
+    out_ref[...] = total.T
 
 
 def run_corr(place, stored, weights, owners):
@@ -590,7 +601,7 @@
         grid_spec=grid_spec,
         out_shape=jax.ShapeDtypeStruct((owners, span, block), jnp.float32),
         compiler_params=params(40 * 2**20),
-        cost_estimate=cost(11),
+        cost_estimate=cost(8),
         name="correlate",
     )(place, stored, weights)
 
@@ -736,19 +747,12 @@
                 table_of.append((i * n_space + j, to * n_space + i // per))
         sent[step] = lax.ppermute(blocks[step], ("tm", "space"), table_of)
     partial = run_corr(place, stored, weights, n_space)
-    partial, *sent = lax.optimization_barrier((partial, *sent))
-    sums = {d: partial[d] for d in range(n_space)}
-
-    bit = 1
-    while bit < n_space:
-        going = [d for d in sums if d & bit]
-        partner = [(i, i ^ bit) for i in range(n_space)]
-        came = lax.ppermute(jnp.stack([sums[d] for d in going]), "space", partner)
-        for n, d in enumerate(going):
-            sums[d ^ bit] = sums[d ^ bit] + came[n]
-            del sums[d]
-        bit *= 2
-    correlations = sums[0].T[None]
+    partial, *sent[:-1] = lax.optimization_barrier((partial, *sent[:-1]))
+    total = partial[0]
+    for distance in range(1, n_space):
+        partner = [(i, i ^ distance) for i in range(n_space)]
+        total = total + lax.ppermute(partial[distance], "space", partner)
+    correlations = total.T[None]
 
     shape = (per, n_space * layers, planes // n_tm, comps * vectors)
     return correlations, run_arrange(place, order, sent, shape, layers, per)

time: 67.3 us -> 65.9 us (0.979)
  the two profiles are of different devices: /device:TPU:0 before, /device:TPU:12 now
where the time goes in v2:
time: 65.9 us; the launch traced here: 64.8 us
  Pallas kernels  38.2 us (58%)
  starting transfers between devices  17.2 us (26%)
  waiting for transfers between devices  7.9 us (12%)
  between operations  0.77 us (1%)
    pallas_call x1, Pallas kernels, run_outer(): pl.pallas_call(functools.partial(outer_kernel, layers=layers, parts=parts...  16 us
    ppermute x4, starting transfers between devices, shards(): sent[step] = lax.ppermute(blocks[step], ('tm', 'space'), table_of)  9.14 us
    pallas_call x1, Pallas kernels, run_inner(): pl.pallas_call(functools.partial(inner_kernel, layers=layers), in_specs=[...  7.96 us
    pallas_call x1, Pallas kernels, run_corr(): pl.pallas_call(functools.partial(corr_kernel, layers=layers), grid_spec=g...  7.7 us
    ppermute x4, waiting for transfers between devices, shards(): sent[step] = lax.ppermute(blocks[step], ('tm', 'space'), table_of)  4.79 us
    ppermute x3, starting transfers between devices, shards(): total = total + lax.ppermute(partial[distance], 'space', partner)  3.83 us
    pallas_call x1, Pallas kernels, run_pack(): pl.pallas_call(functools.partial(pack_kernel, layers=layers, tiles=tiles)...  2.85 us
    pallas_call x1, Pallas kernels, run_arrange(): pl.pallas_call(functools.partial(arrange_kernel, layers=layers, per=per),...  2.16 us
  transfers between devices with their start and end apart: 12, of which 4 were waited for; matrix products, arithmetic and copies ran while one was open for 0% of the time, Pallas kernels for 30%

profile of v2, /device:TPU:12, one launch (start us, length us, event | category | flops | bytes accessed | tf_op | source)
XLA Modules:
  0.0 64.8 jit_solution(17675909734358180597)
XLA Ops:
  0.6 2.8 %pack.1 = (bf16[4,54,256]{2,1,0:T(8,128)(2,1)}, bf16[4,54,256]{2,1,0:T(8,128)(2,1)}, bf16[4,2,6,16,256]{4,3,2,1,0:T(8,128)(2,1)}, bf16[4,2,6,16,256]{4,3,2,1,0:T(8,128)(2,1)}) custom-call(f32[6,512,128]{2,1,0:T(8,128)} %bitcast.35, f32[864,128]{1,0:T(8,128)} %bitcast.37), custom_call_target="tpu_custom_call" | custom-call | flops 1000000 | bytes 7500000 | tf_op jit(solution)/shard_map/pack/pallas_call | solution.py:98
  3.5 0.1 collective-permute-start
  3.6 1.7 %collective-permute-start.1 = (bf16[4,2,6,16,256]{4,3,2,1,0:T(8,128)(2,1)}, bf16[4,2,6,16,256]{4,3,2,1,0:T(8,128)(2,1)S(1)}, u32[]{:S(2)}, u32[]{:S(2)}) collective-permute-start(bf16[4,2,6,16,256]{4,3,2,1,0:T(8,128)(2,1)} %get-tuple-element.25), channel_id=1, source_target_pairs={{1,0},{2,1},{3,2},{0,3},{5,4},{6,5},{7,6},{4,7},{9,8},{10,9},{11,1... | collective-permute-start | bytes 1179656 | tf_op jit(solution)/shard_map/ppermute | solution.py:729
  5.3 1.7 %collective-permute-start.3 = (bf16[4,54,256]{2,1,0:T(8,128)(2,1)}, bf16[4,54,256]{2,1,0:T(8,128)(2,1)S(1)}, u32[]{:S(2)}, u32[]{:S(2)}) collective-permute-start(bf16[4,54,256]{2,1,0:T(8,128)(2,1)} %get-tuple-element.28), channel_id=1, source_target_pairs={{1,0},{2,1},{3,2},{0,3},{5,4},{6,5},{7,6},{4,7},{9,8},{10,9},{11,1... | collective-permute-start | bytes 331784 | tf_op jit(solution)/shard_map/ppermute | solution.py:727
  7.1 0.1 stack.23.place_ref
  7.1 8.0 %inner.1 = (f32[2,16,6,16,256]{4,3,2,1,0:T(8,128)S(1)}, f32[2,16,6,16,256]{4,3,2,1,0:T(8,128)S(1)}, f32[16,112,256]{2,1,0:T(8,128)S(1)}, f32[16,24,256]{2,1,0:T(8,128)S(1)}, f32[24,256]{1,0:T(8,128)S(1)}) custom-call(f32[6,512,128]{2,1,0:T(8,128)S(1)} %bitcast.36, f32[864,128]{1,0:T(8,128)S(1)} %bitcast.38), custom_call_target="tpu_custom_call" | custom-call | flops 1000000 | bytes 24000000 | tf_op jit(solution)/shard_map/inner/pallas_call | solution.py:431
  15.1 1.8 %collective-permute-done.2.lo_ref = bf16[4,54,256]{2,1,0:T(8,128)(2,1)S(1)} collective-permute-done((bf16[4,54,256]{2,1,0:T(8,128)(2,1)}, bf16[4,54,256]{2,1,0:T(8,128)(2,1)S(1)}, u32[]{:S(2)}, u32[]{:S(2)}) %collective-permute-start.2) | collective-permute-done | bytes 110624 | tf_op jit(solution)/shard_map/ppermute | solution.py:726
  16.9 1.2 %gauge_halo.1 = (f32[16,112,256]{2,1,0:T(8,128)S(1)}, f32[16,24,256]{2,1,0:T(8,128)S(1)}) custom-call(f32[24,256]{1,0:T(8,128)S(1)} %get-tuple-element.26.top_ref, bf16[4,54,256]{2,1,0:T(8,128)(2,1)S(1)} %collective-permute-done.2.lo_ref, bf16[4,54,256]{2,1,0:T(8,128)(2,1)S(1)} %collective-permute-done.3.hi_ref, ...), custom_call_target="tpu_custom_call" | custom-call | flops 1000000 | bytes 4500000 | tf_op jit(solution)/shard_map/gauge_halo/pallas_call | solution.py:288
  18.1 16.0 %outer.1 = (bf16[2,8,6,16,256]{4,3,2,1,0:T(8,128)(2,1)S(1)}, bf16[4,2,6,32,128]{4,3,2,1,0:T(8,128)(2,1)S(1)}, bf16[4,2,6,32,128]{4,3,2,1,0:T(8,128)(2,1)S(1)}) custom-call(s32[5]{0:T(128)S(1)} %stack.23.place_ref, bf16[4,2,6,16,256]{4,3,2,1,0:T(8,128)(2,1)S(1)} %collective-permute-done.lo_ref, bf16[4,2,6,16,256]{4,3,2,1,0:T(8,128)(2,1)S(1)} %collective-permute-done.1.hi_ref, ...), custom_call_target="tpu_custom_call" | custom-call | flops 1000000 | bytes 48000000 | tf_op jit(solution)/shard_map/outer/pallas_call | solution.py:513
  34.1 0.7 %collective-permute-start.4 = (bf16[4,2,6,32,128]{4,3,2,1,0:T(8,128)(2,1)S(1)}, bf16[4,2,6,32,128]{4,3,2,1,0:T(8,128)(2,1)S(1)}, u32[]{:S(2)}, u32[]{:S(2)}) collective-permute-start(bf16[4,2,6,32,128]{4,3,2,1,0:T(8,128)(2,1)S(1)} %get-tuple-element.37), channel_id=1, source_target_pairs={{0,1},{1,0},{2,3},{3,2},{4,5},{5,4},{6,7},{7,6},{8,9},{9,8},{10,11... | collective-permute-start | bytes 1179656 | tf_op jit(solution)/shard_map/ppermute | solution.py:737
  34.7 1.3 %collective-permute-done.4.got_ref = bf16[4,2,6,32,128]{4,3,2,1,0:T(8,128)(2,1)S(1)} collective-permute-done((bf16[4,2,6,32,128]{4,3,2,1,0:T(8,128)(2,1)S(1)}, bf16[4,2,6,32,128]{4,3,2,1,0:T(8,128)(2,1)S(1)}, u32[]{:S(2)}, u32[]{:S(2)}) %collective-permute-start.4) | collective-permute-done | bytes 393248 | tf_op jit(solution)/shard_map/ppermute | solution.py:737
  36.1 1.9 %collective-permute-start.5 = (bf16[2,2,6,32,128]{4,3,2,1,0:T(8,128)(2,1)S(1)}, bf16[2,2,6,32,128]{4,3,2,1,0:T(8,128)(2,1)S(1)}, u32[]{:S(2)}, u32[]{:S(2)}) collective-permute-start(bf16[2,2,6,32,128]{4,3,2,1,0:T(8,128)(2,1)S(1)} %get-tuple-element.38), channel_id=1, source_target_pairs={{0,0},{1,16},{2,8},{3,24},{4,4},{5,20},{6,12},{7,28},{8,9},{9,25},... | collective-permute-start | bytes 589832 | tf_op jit(solution)/shard_map/ppermute | solution.py:748
  38.1 3.7 %collective-permute-start.6 = (bf16[2,2,6,32,128]{4,3,2,1,0:T(8,128)(2,1)S(1)}, bf16[2,2,6,32,128]{4,3,2,1,0:T(8,128)(2,1)S(1)}, u32[]{:S(2)}, u32[]{:S(2)}) collective-permute-start(bf16[2,2,6,32,128]{4,3,2,1,0:T(8,128)(2,1)S(1)} %get-tuple-element.39), channel_id=1, source_target_pairs={{0,4},{1,20},{2,12},{3,28},{4,0},{5,16},{6,8},{7,24},{8,13},{9,29}... | collective-permute-start | bytes 589832 | tf_op jit(solution)/shard_map/ppermute | solution.py:748
  41.7 3.0 %collective-permute-start.7 = (bf16[2,2,6,32,128]{4,3,2,1,0:T(8,128)(2,1)S(1)}, bf16[2,2,6,32,128]{4,3,2,1,0:T(8,128)(2,1)S(1)}, u32[]{:S(2)}, u32[]{:S(2)}) collective-permute-start(bf16[2,2,6,32,128]{4,3,2,1,0:T(8,128)(2,1)S(1)} %get-tuple-element.40), channel_id=1, source_target_pairs={{0,8},{1,24},{2,0},{3,16},{4,12},{5,28},{6,4},{7,20},{8,1},{9,17},... | collective-permute-start | bytes 589832 | tf_op jit(solution)/shard_map/ppermute | solution.py:748
  44.7 0.1 weights.1.weight_ref
  44.9 7.7 %correlate.1 = f32[4,64,112]{2,1,0:T(8,128)S(1)} custom-call(s32[5]{0:T(128)S(1)} %stack.23.place_ref, bf16[448,6,8,256]{3,2,1,0:T(8,128)(2,1)S(1)} %bitcast.34, bf16[512,1536]{1,0:T(8,128)(2,1)S(1)} %weights.1.weight_ref), custom_call_target="tpu_custom_call" | custom-call | flops 1000000 | bytes 24000000 | tf_op jit(solution)/shard_map/correlate/pallas_call | solution.py:599
  52.6 0.5 collective-permute-start.11
  53.1 1.8 %collective-permute-done.7.refs_2_ = bf16[2,2,6,32,128]{4,3,2,1,0:T(8,128)(2,1)S(1)} collective-permute-done((bf16[2,2,6,32,128]{4,3,2,1,0:T(8,128)(2,1)S(1)}, bf16[2,2,6,32,128]{4,3,2,1,0:T(8,128)(2,1)S(1)}, u32[]{:S(2)}, u32[]{:S(2)}) %collective-permute-start.7) | collective-permute-done | bytes 196640 | tf_op jit(solution)/shard_map/ppermute | solution.py:748
  55.0 0.1 collective-permute-start.10
  55.0 3.8 %collective-permute-start.9 = (f32[64,112]{1,0:T(8,128)S(1)}, f32[64,112]{1,0:T(8,128)S(1)}, u32[]{:S(2)}, u32[]{:S(2)}) collective-permute-start(f32[64,112]{1,0:T(8,128)S(1)} %get-tuple-element.48), channel_id=1, source_target_pairs={{0,2},{1,3},{2,0},{3,1},{4,6},{5,7},{6,4},{7,5},{8,10},{9,11},{10,... | collective-permute-start | bytes 86024 | tf_op jit(solution)/shard_map/ppermute | solution.py:754
  58.8 0.2 order.1.order_ref
  59.1 2.9 %collective-permute-done.11.refs_3_ = bf16[2,2,6,32,128]{4,3,2,1,0:T(8,128)(2,1)S(1)} collective-permute-done((bf16[2,2,6,32,128]{4,3,2,1,0:T(8,128)(2,1)S(1)}, bf16[2,2,6,32,128]{4,3,2,1,0:T(8,128)(2,1)S(1)}, u32[]{:S(2)}, u32[]{:S(2)}) %collective-permute-start.11) | collective-permute-done | bytes 196640 | tf_op jit(solution)/shard_map/ppermute | solution.py:748
  62.0 2.2 %arrange.1 = bf16[2,32,32,192]{3,2,1,0:T(8,128)(2,1)} custom-call(s32[5]{0:T(128)S(1)} %stack.23.place_ref, bf16[512,512]{1,0:T(8,128)(2,1)S(1)} %order.1.order_ref, bf16[2,2,6,32,128]{4,3,2,1,0:T(8,128)(2,1)S(1)} %collective-permute-done.5.refs_0_, bf16[2,2,6,32,128]{4,3,2,1,0:T(8,128)(2,1)S(1)} %collective-permute-done.6.refs_1_, ...), custom_call_target="tpu_custom_call" | custom-call | flops 1000000 | bytes 9000000 | tf_op jit(solution)/shard_map/arrange/pallas_call | solution.py:682
  64.2 0.6 fusion.2
  (18 shorter events, 0.1 us)
Async XLA Ops:
  0.6 6.5 %copy-start.1 = (f32[1,2,3,32,8,256]{5,4,3,2,1,0:T(8,128)S(1)}, f32[1,2,3,32,8,256]{5,4,3,2,1,0:T(8,128)}, u32[]{:S(2)}) copy-start(f32[1,2,3,32,8,256]{5,4,3,2,1,0:T(8,128)} %param.3) | copy-start | bytes 4718596
  0.6 6.5 %copy-start.2 = (f32[1,3,2,3,3,8,256]{6,5,4,3,2,1,0:T(8,128)S(1)}, f32[1,3,2,3,3,8,256]{6,5,4,3,2,1,0:T(8,128)}, u32[]{:S(2)}) copy-start(f32[1,3,2,3,3,8,256]{6,5,4,3,2,1,0:T(8,128)} %param.4) | copy-start | bytes 1327108
  3.5 14.5 %collective-permute-start = (bf16[4,2,6,16,256]{4,3,2,1,0:T(8,128)(2,1)}, bf16[4,2,6,16,256]{4,3,2,1,0:T(8,128)(2,1)S(1)}, u32[]{:S(2)}, u32[]{:S(2)}) collective-permute-start(bf16[4,2,6,16,256]{4,3,2,1,0:T(8,128)(2,1)} %get-tuple-element.24), channel_id=1, source_target_pairs={{0,1},{1,2},{2,3},{3,0},{4,5},{5,6},{6,7},{7,4},{8,9},{9,10},{10,1... | collective-permute-start | bytes 1179656 | tf_op jit(solution)/shard_map/ppermute | solution.py:728
  3.6 14.5 %collective-permute-start.1 = (bf16[4,2,6,16,256]{4,3,2,1,0:T(8,128)(2,1)}, bf16[4,2,6,16,256]{4,3,2,1,0:T(8,128)(2,1)S(1)}, u32[]{:S(2)}, u32[]{:S(2)}) collective-permute-start(bf16[4,2,6,16,256]{4,3,2,1,0:T(8,128)(2,1)} %get-tuple-element.25), channel_id=1, source_target_pairs={{1,0},{2,1},{3,2},{0,3},{5,4},{6,5},{7,6},{4,7},{9,8},{10,9},{11,1... | collective-permute-start | bytes 1179656 | tf_op jit(solution)/shard_map/ppermute | solution.py:729
  5.3 11.6 %collective-permute-start.2 = (bf16[4,54,256]{2,1,0:T(8,128)(2,1)}, bf16[4,54,256]{2,1,0:T(8,128)(2,1)S(1)}, u32[]{:S(2)}, u32[]{:S(2)}) collective-permute-start(bf16[4,54,256]{2,1,0:T(8,128)(2,1)} %get-tuple-element.27), channel_id=1, source_target_pairs={{0,1},{1,2},{2,3},{3,0},{4,5},{5,6},{6,7},{7,4},{8,9},{9,10},{10,1... | collective-permute-start | bytes 331784 | tf_op jit(solution)/shard_map/ppermute | solution.py:726
  5.3 11.6 %collective-permute-start.3 = (bf16[4,54,256]{2,1,0:T(8,128)(2,1)}, bf16[4,54,256]{2,1,0:T(8,128)(2,1)S(1)}, u32[]{:S(2)}, u32[]{:S(2)}) collective-permute-start(bf16[4,54,256]{2,1,0:T(8,128)(2,1)} %get-tuple-element.28), channel_id=1, source_target_pairs={{1,0},{2,1},{3,2},{0,3},{5,4},{6,5},{7,6},{4,7},{9,8},{10,9},{11,1... | collective-permute-start | bytes 331784 | tf_op jit(solution)/shard_map/ppermute | solution.py:727
  18.1 26.8 %copy-start = (bf16[1,448,2,3,8,256]{5,4,3,2,1,0:T(8,128)(2,1)S(1)}, bf16[1,448,2,3,8,256]{5,4,3,2,1,0:T(8,128)(2,1)}, u32[]{:S(2)}) copy-start(bf16[1,448,2,3,8,256]{5,4,3,2,1,0:T(8,128)(2,1)} %param.5) | copy-start | bytes 33030148
  34.1 2.0 %collective-permute-start.4 = (bf16[4,2,6,32,128]{4,3,2,1,0:T(8,128)(2,1)S(1)}, bf16[4,2,6,32,128]{4,3,2,1,0:T(8,128)(2,1)S(1)}, u32[]{:S(2)}, u32[]{:S(2)}) collective-permute-start(bf16[4,2,6,32,128]{4,3,2,1,0:T(8,128)(2,1)S(1)} %get-tuple-element.37), channel_id=1, source_target_pairs={{0,1},{1,0},{2,3},{3,2},{4,5},{5,4},{6,7},{7,6},{8,9},{9,8},{10,11... | collective-permute-start | bytes 1179656 | tf_op jit(solution)/shard_map/ppermute | solution.py:737
  36.1 17.0 %collective-permute-start.5 = (bf16[2,2,6,32,128]{4,3,2,1,0:T(8,128)(2,1)S(1)}, bf16[2,2,6,32,128]{4,3,2,1,0:T(8,128)(2,1)S(1)}, u32[]{:S(2)}, u32[]{:S(2)}) collective-permute-start(bf16[2,2,6,32,128]{4,3,2,1,0:T(8,128)(2,1)S(1)} %get-tuple-element.38), channel_id=1, source_target_pairs={{0,0},{1,16},{2,8},{3,24},{4,4},{5,20},{6,12},{7,28},{8,9},{9,25},... | collective-permute-start | bytes 589832 | tf_op jit(solution)/shard_map/ppermute | solution.py:748
  38.1 15.1 %collective-permute-start.6 = (bf16[2,2,6,32,128]{4,3,2,1,0:T(8,128)(2,1)S(1)}, bf16[2,2,6,32,128]{4,3,2,1,0:T(8,128)(2,1)S(1)}, u32[]{:S(2)}, u32[]{:S(2)}) collective-permute-start(bf16[2,2,6,32,128]{4,3,2,1,0:T(8,128)(2,1)S(1)} %get-tuple-element.39), channel_id=1, source_target_pairs={{0,4},{1,20},{2,12},{3,28},{4,0},{5,16},{6,8},{7,24},{8,13},{9,29}... | collective-permute-start | bytes 589832 | tf_op jit(solution)/shard_map/ppermute | solution.py:748
  41.7 13.2 %collective-permute-start.7 = (bf16[2,2,6,32,128]{4,3,2,1,0:T(8,128)(2,1)S(1)}, bf16[2,2,6,32,128]{4,3,2,1,0:T(8,128)(2,1)S(1)}, u32[]{:S(2)}, u32[]{:S(2)}) collective-permute-start(bf16[2,2,6,32,128]{4,3,2,1,0:T(8,128)(2,1)S(1)} %get-tuple-element.40), channel_id=1, source_target_pairs={{0,8},{1,24},{2,0},{3,16},{4,12},{5,28},{6,4},{7,20},{8,1},{9,17},... | collective-permute-start | bytes 589832 | tf_op jit(solution)/shard_map/ppermute | solution.py:748
  52.6 9.4 %collective-permute-start.11 = (bf16[2,2,6,32,128]{4,3,2,1,0:T(8,128)(2,1)S(1)}, bf16[2,2,6,32,128]{4,3,2,1,0:T(8,128)(2,1)S(1)}, u32[]{:S(2)}, u32[]{:S(2)}) collective-permute-start(bf16[2,2,6,32,128]{4,3,2,1,0:T(8,128)(2,1)S(1)} %get-tuple-element.45), channel_id=1, source_target_pairs={{0,12},{1,28},{2,4},{3,20},{4,8},{5,24},{6,0},{7,16},{8,5},{9,21},... | collective-permute-start | bytes 589832 | tf_op jit(solution)/shard_map/ppermute | solution.py:748
  55.0 9.2 %collective-permute-start.10 = (f32[64,112]{1,0:T(8,128)S(1)}, f32[64,112]{1,0:T(8,128)S(1)}, u32[]{:S(2)}, u32[]{:S(2)}) collective-permute-start(f32[64,112]{1,0:T(8,128)S(1)} %get-tuple-element.47), channel_id=1, source_target_pairs={{0,3},{1,2},{2,1},{3,0},{4,7},{5,6},{6,5},{7,4},{8,11},{9,10},{10,... | collective-permute-start | bytes 86024 | tf_op jit(solution)/shard_map/ppermute | solution.py:754
  55.0 9.1 %collective-permute-start.9 = (f32[64,112]{1,0:T(8,128)S(1)}, f32[64,112]{1,0:T(8,128)S(1)}, u32[]{:S(2)}, u32[]{:S(2)}) collective-permute-start(f32[64,112]{1,0:T(8,128)S(1)} %get-tuple-element.48), channel_id=1, source_target_pairs={{0,2},{1,3},{2,0},{3,1},{4,6},{5,7},{6,4},{7,5},{8,10},{9,11},{10,... | collective-permute-start | bytes 86024 | tf_op jit(solution)/shard_map/ppermute | solution.py:754
  58.8 5.4 %collective-permute-start.8 = (f32[64,112]{1,0:T(8,128)S(1)}, f32[64,112]{1,0:T(8,128)S(1)}, u32[]{:S(2)}, u32[]{:S(2)}) collective-permute-start(f32[64,112]{1,0:T(8,128)S(1)} %get-tuple-element.46), channel_id=1, source_target_pairs={{0,1},{1,0},{2,3},{3,2},{4,5},{5,4},{6,7},{7,6},{8,9},{9,8},{10,11... | collective-permute-start | bytes 86024 | tf_op jit(solution)/shard_map/ppermute | solution.py:754

commit v3 on v2

--- a/solution.py
+++ b/solution.py
@@ -467,18 +467,20 @@
         src, dst = (a_ref, b_ref) if level % 2 else (b_ref, a_ref)
 
         def body(n, _, src=src, dst=dst, level=level):
-            g, at = n // DEGREE, n % DEGREE
-            for x in (level + at, total - DEGREE - level + at):
-                put(dst, g, x, layer(table_ref, g, x, src, dst, level == 1, tiles))
+            steps = DEGREE // 2
+            g, at = n // steps, 2 * (n % steps)
+            for first in (level + at, total - DEGREE - level + at):
+                for x in (first, first + 1):
+                    put(dst, g, x, layer(table_ref, g, x, src, dst, level == 1, tiles))
             return 0
 
-        lax.fori_loop(0, groups * DEGREE, body, 0)
+        lax.fori_loop(0, groups * (DEGREE // 2), body, 0)
     src, prev = (a_ref, b_ref) if DEGREE % 2 else (b_ref, a_ref)
 
     def last(n, _):
-        g, at = n // (layers // 2), n % (layers // 2)
-        for u in range(2):
-            x = 2 * at + u
+        g, at = n // (layers // 4), n % (layers // 4)
+        for u in range(4):
+            x = 4 * at + u
             value = layer(table_ref, g, x + DEGREE, src, prev, False, tiles)
             value = turn(gauge_ref, x + DEGREE, lambda k, t: value[k, t], True, tiles)
             for (k, t), v in value.items():
@@ -489,7 +491,7 @@
                 )
         return 0
 
-    lax.fori_loop(0, groups * (layers // 2), last, 0)
+    lax.fori_loop(0, groups * (layers // 4), last, 0)
 
     side, base = place_ref[0], place_ref[1]
     pairs = parts // 2

time: 65.9 us -> 64.6 us (0.980)
  Pallas kernels: 38.2 us -> 36.9 us
    pallas_call x1, Pallas kernels: 16 us -> 14.7 us  [run_outer(): pl.pallas_call(functools.partial(outer_kernel, layers=layers, parts=parts...]
where the time goes in v3:
time: 64.6 us; the launch traced here: 63.5 us
  Pallas kernels  36.9 us (57%)
  starting transfers between devices  17.2 us (27%)
  waiting for transfers between devices  7.91 us (12%)
  between operations  0.77 us (1%)
    pallas_call x1, Pallas kernels, run_outer(): pl.pallas_call(functools.partial(outer_kernel, layers=layers, parts=parts...  14.7 us
    ppermute x4, starting transfers between devices, shards(): sent[step] = lax.ppermute(blocks[step], ('tm', 'space'), table_of)  9.14 us
    pallas_call x1, Pallas kernels, run_inner(): pl.pallas_call(functools.partial(inner_kernel, layers=layers), in_specs=[...  7.96 us
    pallas_call x1, Pallas kernels, run_corr(): pl.pallas_call(functools.partial(corr_kernel, layers=layers), grid_spec=g...  7.7 us
    ppermute x4, waiting for transfers between devices, shards(): sent[step] = lax.ppermute(blocks[step], ('tm', 'space'), table_of)  4.79 us
    ppermute x3, starting transfers between devices, shards(): total = total + lax.ppermute(partial[distance], 'space', partner)  3.83 us
    pallas_call x1, Pallas kernels, run_pack(): pl.pallas_call(functools.partial(pack_kernel, layers=layers, tiles=tiles)...  2.85 us
    pallas_call x1, Pallas kernels, run_arrange(): pl.pallas_call(functools.partial(arrange_kernel, layers=layers, per=per),...  2.16 us
  transfers between devices with their start and end apart: 12, of which 4 were waited for; matrix products, arithmetic and copies ran while one was open for 0% of the time, Pallas kernels for 30%

profile of v3, /device:TPU:12, one launch (start us, length us, event | category | flops | bytes accessed | tf_op | source)
XLA Modules:
  0.0 63.5 jit_solution(17581942379859671665)
XLA Ops:
  0.6 2.8 %pack.1 = (bf16[4,54,256]{2,1,0:T(8,128)(2,1)}, bf16[4,54,256]{2,1,0:T(8,128)(2,1)}, bf16[4,2,6,16,256]{4,3,2,1,0:T(8,128)(2,1)}, bf16[4,2,6,16,256]{4,3,2,1,0:T(8,128)(2,1)}) custom-call(f32[6,512,128]{2,1,0:T(8,128)} %bitcast.35, f32[864,128]{1,0:T(8,128)} %bitcast.37), custom_call_target="tpu_custom_call" | custom-call | flops 1000000 | bytes 7500000 | tf_op jit(solution)/shard_map/pack/pallas_call | solution.py:98
  3.5 0.1 collective-permute-start
  3.6 1.7 %collective-permute-start.1 = (bf16[4,2,6,16,256]{4,3,2,1,0:T(8,128)(2,1)}, bf16[4,2,6,16,256]{4,3,2,1,0:T(8,128)(2,1)S(1)}, u32[]{:S(2)}, u32[]{:S(2)}) collective-permute-start(bf16[4,2,6,16,256]{4,3,2,1,0:T(8,128)(2,1)} %get-tuple-element.25), channel_id=1, source_target_pairs={{1,0},{2,1},{3,2},{0,3},{5,4},{6,5},{7,6},{4,7},{9,8},{10,9},{11,1... | collective-permute-start | bytes 1179656 | tf_op jit(solution)/shard_map/ppermute | solution.py:731
  5.3 1.7 %collective-permute-start.3 = (bf16[4,54,256]{2,1,0:T(8,128)(2,1)}, bf16[4,54,256]{2,1,0:T(8,128)(2,1)S(1)}, u32[]{:S(2)}, u32[]{:S(2)}) collective-permute-start(bf16[4,54,256]{2,1,0:T(8,128)(2,1)} %get-tuple-element.28), channel_id=1, source_target_pairs={{1,0},{2,1},{3,2},{0,3},{5,4},{6,5},{7,6},{4,7},{9,8},{10,9},{11,1... | collective-permute-start | bytes 331784 | tf_op jit(solution)/shard_map/ppermute | solution.py:729
  7.1 0.1 stack.23.place_ref
  7.1 8.0 %inner.1 = (f32[2,16,6,16,256]{4,3,2,1,0:T(8,128)S(1)}, f32[2,16,6,16,256]{4,3,2,1,0:T(8,128)S(1)}, f32[16,112,256]{2,1,0:T(8,128)S(1)}, f32[16,24,256]{2,1,0:T(8,128)S(1)}, f32[24,256]{1,0:T(8,128)S(1)}) custom-call(f32[6,512,128]{2,1,0:T(8,128)S(1)} %bitcast.36, f32[864,128]{1,0:T(8,128)S(1)} %bitcast.38), custom_call_target="tpu_custom_call" | custom-call | flops 1000000 | bytes 24000000 | tf_op jit(solution)/shard_map/inner/pallas_call | solution.py:431
  15.1 1.8 %collective-permute-done.2.lo_ref = bf16[4,54,256]{2,1,0:T(8,128)(2,1)S(1)} collective-permute-done((bf16[4,54,256]{2,1,0:T(8,128)(2,1)}, bf16[4,54,256]{2,1,0:T(8,128)(2,1)S(1)}, u32[]{:S(2)}, u32[]{:S(2)}) %collective-permute-start.2) | collective-permute-done | bytes 110624 | tf_op jit(solution)/shard_map/ppermute | solution.py:728
  16.9 1.2 %gauge_halo.1 = (f32[16,112,256]{2,1,0:T(8,128)S(1)}, f32[16,24,256]{2,1,0:T(8,128)S(1)}) custom-call(f32[24,256]{1,0:T(8,128)S(1)} %get-tuple-element.26.top_ref, bf16[4,54,256]{2,1,0:T(8,128)(2,1)S(1)} %collective-permute-done.2.lo_ref, bf16[4,54,256]{2,1,0:T(8,128)(2,1)S(1)} %collective-permute-done.3.hi_ref, ...), custom_call_target="tpu_custom_call" | custom-call | flops 1000000 | bytes 4500000 | tf_op jit(solution)/shard_map/gauge_halo/pallas_call | solution.py:288
  18.1 14.7 %outer.1 = (bf16[2,8,6,16,256]{4,3,2,1,0:T(8,128)(2,1)S(1)}, bf16[4,2,6,32,128]{4,3,2,1,0:T(8,128)(2,1)S(1)}, bf16[4,2,6,32,128]{4,3,2,1,0:T(8,128)(2,1)S(1)}) custom-call(s32[5]{0:T(128)S(1)} %stack.23.place_ref, bf16[4,2,6,16,256]{4,3,2,1,0:T(8,128)(2,1)S(1)} %collective-permute-done.lo_ref, bf16[4,2,6,16,256]{4,3,2,1,0:T(8,128)(2,1)S(1)} %collective-permute-done.1.hi_ref, ...), custom_call_target="tpu_custom_call" | custom-call | flops 1000000 | bytes 48000000 | tf_op jit(solution)/shard_map/outer/pallas_call | solution.py:515
  32.8 0.7 %collective-permute-start.4 = (bf16[4,2,6,32,128]{4,3,2,1,0:T(8,128)(2,1)S(1)}, bf16[4,2,6,32,128]{4,3,2,1,0:T(8,128)(2,1)S(1)}, u32[]{:S(2)}, u32[]{:S(2)}) collective-permute-start(bf16[4,2,6,32,128]{4,3,2,1,0:T(8,128)(2,1)S(1)} %get-tuple-element.37), channel_id=1, source_target_pairs={{0,1},{1,0},{2,3},{3,2},{4,5},{5,4},{6,7},{7,6},{8,9},{9,8},{10,11... | collective-permute-start | bytes 1179656 | tf_op jit(solution)/shard_map/ppermute | solution.py:739
  33.4 1.3 %collective-permute-done.4.got_ref = bf16[4,2,6,32,128]{4,3,2,1,0:T(8,128)(2,1)S(1)} collective-permute-done((bf16[4,2,6,32,128]{4,3,2,1,0:T(8,128)(2,1)S(1)}, bf16[4,2,6,32,128]{4,3,2,1,0:T(8,128)(2,1)S(1)}, u32[]{:S(2)}, u32[]{:S(2)}) %collective-permute-start.4) | collective-permute-done | bytes 393248 | tf_op jit(solution)/shard_map/ppermute | solution.py:739
  34.8 1.9 %collective-permute-start.5 = (bf16[2,2,6,32,128]{4,3,2,1,0:T(8,128)(2,1)S(1)}, bf16[2,2,6,32,128]{4,3,2,1,0:T(8,128)(2,1)S(1)}, u32[]{:S(2)}, u32[]{:S(2)}) collective-permute-start(bf16[2,2,6,32,128]{4,3,2,1,0:T(8,128)(2,1)S(1)} %get-tuple-element.38), channel_id=1, source_target_pairs={{0,0},{1,16},{2,8},{3,24},{4,4},{5,20},{6,12},{7,28},{8,9},{9,25},... | collective-permute-start | bytes 589832 | tf_op jit(solution)/shard_map/ppermute | solution.py:750
  36.8 3.7 %collective-permute-start.6 = (bf16[2,2,6,32,128]{4,3,2,1,0:T(8,128)(2,1)S(1)}, bf16[2,2,6,32,128]{4,3,2,1,0:T(8,128)(2,1)S(1)}, u32[]{:S(2)}, u32[]{:S(2)}) collective-permute-start(bf16[2,2,6,32,128]{4,3,2,1,0:T(8,128)(2,1)S(1)} %get-tuple-element.39), channel_id=1, source_target_pairs={{0,4},{1,20},{2,12},{3,28},{4,0},{5,16},{6,8},{7,24},{8,13},{9,29}... | collective-permute-start | bytes 589832 | tf_op jit(solution)/shard_map/ppermute | solution.py:750
  40.4 3.0 %collective-permute-start.7 = (bf16[2,2,6,32,128]{4,3,2,1,0:T(8,128)(2,1)S(1)}, bf16[2,2,6,32,128]{4,3,2,1,0:T(8,128)(2,1)S(1)}, u32[]{:S(2)}, u32[]{:S(2)}) collective-permute-start(bf16[2,2,6,32,128]{4,3,2,1,0:T(8,128)(2,1)S(1)} %get-tuple-element.40), channel_id=1, source_target_pairs={{0,8},{1,24},{2,0},{3,16},{4,12},{5,28},{6,4},{7,20},{8,1},{9,17},... | collective-permute-start | bytes 589832 | tf_op jit(solution)/shard_map/ppermute | solution.py:750
  43.5 0.1 weights.1.weight_ref
  43.6 7.7 %correlate.1 = f32[4,64,112]{2,1,0:T(8,128)S(1)} custom-call(s32[5]{0:T(128)S(1)} %stack.23.place_ref, bf16[448,6,8,256]{3,2,1,0:T(8,128)(2,1)S(1)} %bitcast.34, bf16[512,1536]{1,0:T(8,128)(2,1)S(1)} %weights.1.weight_ref), custom_call_target="tpu_custom_call" | custom-call | flops 1000000 | bytes 24000000 | tf_op jit(solution)/shard_map/correlate/pallas_call | solution.py:601
  51.3 0.5 collective-permute-start.11
  51.8 1.8 %collective-permute-done.7.refs_2_ = bf16[2,2,6,32,128]{4,3,2,1,0:T(8,128)(2,1)S(1)} collective-permute-done((bf16[2,2,6,32,128]{4,3,2,1,0:T(8,128)(2,1)S(1)}, bf16[2,2,6,32,128]{4,3,2,1,0:T(8,128)(2,1)S(1)}, u32[]{:S(2)}, u32[]{:S(2)}) %collective-permute-start.7) | collective-permute-done | bytes 196640 | tf_op jit(solution)/shard_map/ppermute | solution.py:750
  53.7 0.1 collective-permute-start.10
  53.8 3.8 %collective-permute-start.9 = (f32[64,112]{1,0:T(8,128)S(1)}, f32[64,112]{1,0:T(8,128)S(1)}, u32[]{:S(2)}, u32[]{:S(2)}) collective-permute-start(f32[64,112]{1,0:T(8,128)S(1)} %get-tuple-element.48), channel_id=1, source_target_pairs={{0,2},{1,3},{2,0},{3,1},{4,6},{5,7},{6,4},{7,5},{8,10},{9,11},{10,... | collective-permute-start | bytes 86024 | tf_op jit(solution)/shard_map/ppermute | solution.py:756
  57.5 0.2 order.1.order_ref
  57.8 2.9 %collective-permute-done.11.refs_3_ = bf16[2,2,6,32,128]{4,3,2,1,0:T(8,128)(2,1)S(1)} collective-permute-done((bf16[2,2,6,32,128]{4,3,2,1,0:T(8,128)(2,1)S(1)}, bf16[2,2,6,32,128]{4,3,2,1,0:T(8,128)(2,1)S(1)}, u32[]{:S(2)}, u32[]{:S(2)}) %collective-permute-start.11) | collective-permute-done | bytes 196640 | tf_op jit(solution)/shard_map/ppermute | solution.py:750
  60.7 2.2 %arrange.1 = bf16[2,32,32,192]{3,2,1,0:T(8,128)(2,1)} custom-call(s32[5]{0:T(128)S(1)} %stack.23.place_ref, bf16[512,512]{1,0:T(8,128)(2,1)S(1)} %order.1.order_ref, bf16[2,2,6,32,128]{4,3,2,1,0:T(8,128)(2,1)S(1)} %collective-permute-done.5.refs_0_, bf16[2,2,6,32,128]{4,3,2,1,0:T(8,128)(2,1)S(1)} %collective-permute-done.6.refs_1_, ...), custom_call_target="tpu_custom_call" | custom-call | flops 1000000 | bytes 9000000 | tf_op jit(solution)/shard_map/arrange/pallas_call | solution.py:684
  62.9 0.6 fusion.2
  (18 shorter events, 0.1 us)
Async XLA Ops:
  0.6 6.5 %copy-start.1 = (f32[1,2,3,32,8,256]{5,4,3,2,1,0:T(8,128)S(1)}, f32[1,2,3,32,8,256]{5,4,3,2,1,0:T(8,128)}, u32[]{:S(2)}) copy-start(f32[1,2,3,32,8,256]{5,4,3,2,1,0:T(8,128)} %param.3) | copy-start | bytes 4718596
  0.6 6.5 %copy-start.2 = (f32[1,3,2,3,3,8,256]{6,5,4,3,2,1,0:T(8,128)S(1)}, f32[1,3,2,3,3,8,256]{6,5,4,3,2,1,0:T(8,128)}, u32[]{:S(2)}) copy-start(f32[1,3,2,3,3,8,256]{6,5,4,3,2,1,0:T(8,128)} %param.4) | copy-start | bytes 1327108
  3.5 14.5 %collective-permute-start = (bf16[4,2,6,16,256]{4,3,2,1,0:T(8,128)(2,1)}, bf16[4,2,6,16,256]{4,3,2,1,0:T(8,128)(2,1)S(1)}, u32[]{:S(2)}, u32[]{:S(2)}) collective-permute-start(bf16[4,2,6,16,256]{4,3,2,1,0:T(8,128)(2,1)} %get-tuple-element.24), channel_id=1, source_target_pairs={{0,1},{1,2},{2,3},{3,0},{4,5},{5,6},{6,7},{7,4},{8,9},{9,10},{10,1... | collective-permute-start | bytes 1179656 | tf_op jit(solution)/shard_map/ppermute | solution.py:730
  3.6 14.5 %collective-permute-start.1 = (bf16[4,2,6,16,256]{4,3,2,1,0:T(8,128)(2,1)}, bf16[4,2,6,16,256]{4,3,2,1,0:T(8,128)(2,1)S(1)}, u32[]{:S(2)}, u32[]{:S(2)}) collective-permute-start(bf16[4,2,6,16,256]{4,3,2,1,0:T(8,128)(2,1)} %get-tuple-element.25), channel_id=1, source_target_pairs={{1,0},{2,1},{3,2},{0,3},{5,4},{6,5},{7,6},{4,7},{9,8},{10,9},{11,1... | collective-permute-start | bytes 1179656 | tf_op jit(solution)/shard_map/ppermute | solution.py:731
  5.3 11.6 %collective-permute-start.2 = (bf16[4,54,256]{2,1,0:T(8,128)(2,1)}, bf16[4,54,256]{2,1,0:T(8,128)(2,1)S(1)}, u32[]{:S(2)}, u32[]{:S(2)}) collective-permute-start(bf16[4,54,256]{2,1,0:T(8,128)(2,1)} %get-tuple-element.27), channel_id=1, source_target_pairs={{0,1},{1,2},{2,3},{3,0},{4,5},{5,6},{6,7},{7,4},{8,9},{9,10},{10,1... | collective-permute-start | bytes 331784 | tf_op jit(solution)/shard_map/ppermute | solution.py:728
  5.3 11.6 %collective-permute-start.3 = (bf16[4,54,256]{2,1,0:T(8,128)(2,1)}, bf16[4,54,256]{2,1,0:T(8,128)(2,1)S(1)}, u32[]{:S(2)}, u32[]{:S(2)}) collective-permute-start(bf16[4,54,256]{2,1,0:T(8,128)(2,1)} %get-tuple-element.28), channel_id=1, source_target_pairs={{1,0},{2,1},{3,2},{0,3},{5,4},{6,5},{7,6},{4,7},{9,8},{10,9},{11,1... | collective-permute-start | bytes 331784 | tf_op jit(solution)/shard_map/ppermute | solution.py:729
  18.1 25.5 %copy-start = (bf16[1,448,2,3,8,256]{5,4,3,2,1,0:T(8,128)(2,1)S(1)}, bf16[1,448,2,3,8,256]{5,4,3,2,1,0:T(8,128)(2,1)}, u32[]{:S(2)}) copy-start(bf16[1,448,2,3,8,256]{5,4,3,2,1,0:T(8,128)(2,1)} %param.5) | copy-start | bytes 33030148
  32.8 2.0 %collective-permute-start.4 = (bf16[4,2,6,32,128]{4,3,2,1,0:T(8,128)(2,1)S(1)}, bf16[4,2,6,32,128]{4,3,2,1,0:T(8,128)(2,1)S(1)}, u32[]{:S(2)}, u32[]{:S(2)}) collective-permute-start(bf16[4,2,6,32,128]{4,3,2,1,0:T(8,128)(2,1)S(1)} %get-tuple-element.37), channel_id=1, source_target_pairs={{0,1},{1,0},{2,3},{3,2},{4,5},{5,4},{6,7},{7,6},{8,9},{9,8},{10,11... | collective-permute-start | bytes 1179656 | tf_op jit(solution)/shard_map/ppermute | solution.py:739
  34.8 17.0 %collective-permute-start.5 = (bf16[2,2,6,32,128]{4,3,2,1,0:T(8,128)(2,1)S(1)}, bf16[2,2,6,32,128]{4,3,2,1,0:T(8,128)(2,1)S(1)}, u32[]{:S(2)}, u32[]{:S(2)}) collective-permute-start(bf16[2,2,6,32,128]{4,3,2,1,0:T(8,128)(2,1)S(1)} %get-tuple-element.38), channel_id=1, source_target_pairs={{0,0},{1,16},{2,8},{3,24},{4,4},{5,20},{6,12},{7,28},{8,9},{9,25},... | collective-permute-start | bytes 589832 | tf_op jit(solution)/shard_map/ppermute | solution.py:750
  36.8 15.1 %collective-permute-start.6 = (bf16[2,2,6,32,128]{4,3,2,1,0:T(8,128)(2,1)S(1)}, bf16[2,2,6,32,128]{4,3,2,1,0:T(8,128)(2,1)S(1)}, u32[]{:S(2)}, u32[]{:S(2)}) collective-permute-start(bf16[2,2,6,32,128]{4,3,2,1,0:T(8,128)(2,1)S(1)} %get-tuple-element.39), channel_id=1, source_target_pairs={{0,4},{1,20},{2,12},{3,28},{4,0},{5,16},{6,8},{7,24},{8,13},{9,29}... | collective-permute-start | bytes 589832 | tf_op jit(solution)/shard_map/ppermute | solution.py:750
  40.4 13.2 %collective-permute-start.7 = (bf16[2,2,6,32,128]{4,3,2,1,0:T(8,128)(2,1)S(1)}, bf16[2,2,6,32,128]{4,3,2,1,0:T(8,128)(2,1)S(1)}, u32[]{:S(2)}, u32[]{:S(2)}) collective-permute-start(bf16[2,2,6,32,128]{4,3,2,1,0:T(8,128)(2,1)S(1)} %get-tuple-element.40), channel_id=1, source_target_pairs={{0,8},{1,24},{2,0},{3,16},{4,12},{5,28},{6,4},{7,20},{8,1},{9,17},... | collective-permute-start | bytes 589832 | tf_op jit(solution)/shard_map/ppermute | solution.py:750
  51.3 9.4 %collective-permute-start.11 = (bf16[2,2,6,32,128]{4,3,2,1,0:T(8,128)(2,1)S(1)}, bf16[2,2,6,32,128]{4,3,2,1,0:T(8,128)(2,1)S(1)}, u32[]{:S(2)}, u32[]{:S(2)}) collective-permute-start(bf16[2,2,6,32,128]{4,3,2,1,0:T(8,128)(2,1)S(1)} %get-tuple-element.45), channel_id=1, source_target_pairs={{0,12},{1,28},{2,4},{3,20},{4,8},{5,24},{6,0},{7,16},{8,5},{9,21},... | collective-permute-start | bytes 589832 | tf_op jit(solution)/shard_map/ppermute | solution.py:750
  53.7 9.2 %collective-permute-start.10 = (f32[64,112]{1,0:T(8,128)S(1)}, f32[64,112]{1,0:T(8,128)S(1)}, u32[]{:S(2)}, u32[]{:S(2)}) collective-permute-start(f32[64,112]{1,0:T(8,128)S(1)} %get-tuple-element.47), channel_id=1, source_target_pairs={{0,3},{1,2},{2,1},{3,0},{4,7},{5,6},{6,5},{7,4},{8,11},{9,10},{10,... | collective-permute-start | bytes 86024 | tf_op jit(solution)/shard_map/ppermute | solution.py:756
  53.8 9.1 %collective-permute-start.9 = (f32[64,112]{1,0:T(8,128)S(1)}, f32[64,112]{1,0:T(8,128)S(1)}, u32[]{:S(2)}, u32[]{:S(2)}) collective-permute-start(f32[64,112]{1,0:T(8,128)S(1)} %get-tuple-element.48), channel_id=1, source_target_pairs={{0,2},{1,3},{2,0},{3,1},{4,6},{5,7},{6,4},{7,5},{8,10},{9,11},{10,... | collective-permute-start | bytes 86024 | tf_op jit(solution)/shard_map/ppermute | solution.py:756
  57.5 5.4 %collective-permute-start.8 = (f32[64,112]{1,0:T(8,128)S(1)}, f32[64,112]{1,0:T(8,128)S(1)}, u32[]{:S(2)}, u32[]{:S(2)}) collective-permute-start(f32[64,112]{1,0:T(8,128)S(1)} %get-tuple-element.46), channel_id=1, source_target_pairs={{0,1},{1,0},{2,3},{3,2},{4,5},{5,4},{6,7},{7,6},{8,9},{9,8},{10,11... | collective-permute-start | bytes 86024 | tf_op jit(solution)/shard_map/ppermute | solution.py:756

commit v4 on v3

--- a/solution.py
+++ b/solution.py
@@ -467,14 +467,12 @@
         src, dst = (a_ref, b_ref) if level % 2 else (b_ref, a_ref)
 
         def body(n, _, src=src, dst=dst, level=level):
-            steps = DEGREE // 2
-            g, at = n // steps, 2 * (n % steps)
-            for first in (level + at, total - DEGREE - level + at):
-                for x in (first, first + 1):
-                    put(dst, g, x, layer(table_ref, g, x, src, dst, level == 1, tiles))
+            for at in range(DEGREE):
+                for x in (level + at, total - DEGREE - level + at):
+                    put(dst, n, x, layer(table_ref, n, x, src, dst, level == 1, tiles))
             return 0
 
-        lax.fori_loop(0, groups * (DEGREE // 2), body, 0)
+        lax.fori_loop(0, groups, body, 0)
     src, prev = (a_ref, b_ref) if DEGREE % 2 else (b_ref, a_ref)
 
     def last(n, _):

time: 64.6 us -> 64.1 us (level)
  transfers between devices with their start and end apart: 12 -> 12, of which waited for: 4 -> 4; matrix products, arithmetic and copies ran while one was open for 0% -> 0% of each run, Pallas kernels for 30% -> 31%
where the time goes in v4:
time: 64.1 us; the launch traced here: 63 us
  Pallas kernels  36.4 us (57%)
  starting transfers between devices  17.2 us (27%)
  waiting for transfers between devices  7.91 us (12%)
  between operations  0.77 us (1%)
    pallas_call x1, Pallas kernels, run_outer(): pl.pallas_call(functools.partial(outer_kernel, layers=layers, parts=parts...  14.2 us
    ppermute x4, starting transfers between devices, shards(): sent[step] = lax.ppermute(blocks[step], ('tm', 'space'), table_of)  9.14 us
    pallas_call x1, Pallas kernels, run_inner(): pl.pallas_call(functools.partial(inner_kernel, layers=layers), in_specs=[...  7.96 us
    pallas_call x1, Pallas kernels, run_corr(): pl.pallas_call(functools.partial(corr_kernel, layers=layers), grid_spec=g...  7.7 us
    ppermute x4, waiting for transfers between devices, shards(): sent[step] = lax.ppermute(blocks[step], ('tm', 'space'), table_of)  4.79 us
    ppermute x3, starting transfers between devices, shards(): total = total + lax.ppermute(partial[distance], 'space', partner)  3.83 us
    pallas_call x1, Pallas kernels, run_pack(): pl.pallas_call(functools.partial(pack_kernel, layers=layers, tiles=tiles)...  2.85 us
    pallas_call x1, Pallas kernels, run_arrange(): pl.pallas_call(functools.partial(arrange_kernel, layers=layers, per=per),...  2.16 us
  transfers between devices with their start and end apart: 12, of which 4 were waited for; matrix products, arithmetic and copies ran while one was open for 0% of the time, Pallas kernels for 31%

profile of v4, /device:TPU:12, one launch (start us, length us, event | category | flops | bytes accessed | tf_op | source)
XLA Modules:
  0.0 63.0 jit_solution(1630536469863825316)
XLA Ops:
  0.6 2.8 %pack.1 = (bf16[4,54,256]{2,1,0:T(8,128)(2,1)}, bf16[4,54,256]{2,1,0:T(8,128)(2,1)}, bf16[4,2,6,16,256]{4,3,2,1,0:T(8,128)(2,1)}, bf16[4,2,6,16,256]{4,3,2,1,0:T(8,128)(2,1)}) custom-call(f32[6,512,128]{2,1,0:T(8,128)} %bitcast.35, f32[864,128]{1,0:T(8,128)} %bitcast.37), custom_call_target="tpu_custom_call" | custom-call | flops 1000000 | bytes 7500000 | tf_op jit(solution)/shard_map/pack/pallas_call | solution.py:98
  3.5 0.1 collective-permute-start
  3.6 1.7 %collective-permute-start.1 = (bf16[4,2,6,16,256]{4,3,2,1,0:T(8,128)(2,1)}, bf16[4,2,6,16,256]{4,3,2,1,0:T(8,128)(2,1)S(1)}, u32[]{:S(2)}, u32[]{:S(2)}) collective-permute-start(bf16[4,2,6,16,256]{4,3,2,1,0:T(8,128)(2,1)} %get-tuple-element.25), channel_id=1, source_target_pairs={{1,0},{2,1},{3,2},{0,3},{5,4},{6,5},{7,6},{4,7},{9,8},{10,9},{11,1... | collective-permute-start | bytes 1179656 | tf_op jit(solution)/shard_map/ppermute | solution.py:729
  5.3 1.7 %collective-permute-start.3 = (bf16[4,54,256]{2,1,0:T(8,128)(2,1)}, bf16[4,54,256]{2,1,0:T(8,128)(2,1)S(1)}, u32[]{:S(2)}, u32[]{:S(2)}) collective-permute-start(bf16[4,54,256]{2,1,0:T(8,128)(2,1)} %get-tuple-element.28), channel_id=1, source_target_pairs={{1,0},{2,1},{3,2},{0,3},{5,4},{6,5},{7,6},{4,7},{9,8},{10,9},{11,1... | collective-permute-start | bytes 331784 | tf_op jit(solution)/shard_map/ppermute | solution.py:727
  7.1 0.1 stack.23.place_ref
  7.1 8.0 %inner.1 = (f32[2,16,6,16,256]{4,3,2,1,0:T(8,128)S(1)}, f32[2,16,6,16,256]{4,3,2,1,0:T(8,128)S(1)}, f32[16,112,256]{2,1,0:T(8,128)S(1)}, f32[16,24,256]{2,1,0:T(8,128)S(1)}, f32[24,256]{1,0:T(8,128)S(1)}) custom-call(f32[6,512,128]{2,1,0:T(8,128)S(1)} %bitcast.36, f32[864,128]{1,0:T(8,128)S(1)} %bitcast.38), custom_call_target="tpu_custom_call" | custom-call | flops 1000000 | bytes 24000000 | tf_op jit(solution)/shard_map/inner/pallas_call | solution.py:431
  15.1 1.8 %collective-permute-done.2.lo_ref = bf16[4,54,256]{2,1,0:T(8,128)(2,1)S(1)} collective-permute-done((bf16[4,54,256]{2,1,0:T(8,128)(2,1)}, bf16[4,54,256]{2,1,0:T(8,128)(2,1)S(1)}, u32[]{:S(2)}, u32[]{:S(2)}) %collective-permute-start.2) | collective-permute-done | bytes 110624 | tf_op jit(solution)/shard_map/ppermute | solution.py:726
  16.9 1.2 %gauge_halo.1 = (f32[16,112,256]{2,1,0:T(8,128)S(1)}, f32[16,24,256]{2,1,0:T(8,128)S(1)}) custom-call(f32[24,256]{1,0:T(8,128)S(1)} %get-tuple-element.26.top_ref, bf16[4,54,256]{2,1,0:T(8,128)(2,1)S(1)} %collective-permute-done.2.lo_ref, bf16[4,54,256]{2,1,0:T(8,128)(2,1)S(1)} %collective-permute-done.3.hi_ref, ...), custom_call_target="tpu_custom_call" | custom-call | flops 1000000 | bytes 4500000 | tf_op jit(solution)/shard_map/gauge_halo/pallas_call | solution.py:288
  18.1 14.2 %outer.1 = (bf16[2,8,6,16,256]{4,3,2,1,0:T(8,128)(2,1)S(1)}, bf16[4,2,6,32,128]{4,3,2,1,0:T(8,128)(2,1)S(1)}, bf16[4,2,6,32,128]{4,3,2,1,0:T(8,128)(2,1)S(1)}) custom-call(s32[5]{0:T(128)S(1)} %stack.23.place_ref, bf16[4,2,6,16,256]{4,3,2,1,0:T(8,128)(2,1)S(1)} %collective-permute-done.lo_ref, bf16[4,2,6,16,256]{4,3,2,1,0:T(8,128)(2,1)S(1)} %collective-permute-done.1.hi_ref, ...), custom_call_target="tpu_custom_call" | custom-call | flops 1000000 | bytes 48000000 | tf_op jit(solution)/shard_map/outer/pallas_call | solution.py:513
  32.2 0.7 %collective-permute-start.4 = (bf16[4,2,6,32,128]{4,3,2,1,0:T(8,128)(2,1)S(1)}, bf16[4,2,6,32,128]{4,3,2,1,0:T(8,128)(2,1)S(1)}, u32[]{:S(2)}, u32[]{:S(2)}) collective-permute-start(bf16[4,2,6,32,128]{4,3,2,1,0:T(8,128)(2,1)S(1)} %get-tuple-element.37), channel_id=1, source_target_pairs={{0,1},{1,0},{2,3},{3,2},{4,5},{5,4},{6,7},{7,6},{8,9},{9,8},{10,11... | collective-permute-start | bytes 1179656 | tf_op jit(solution)/shard_map/ppermute | solution.py:737
  32.9 1.3 %collective-permute-done.4.got_ref = bf16[4,2,6,32,128]{4,3,2,1,0:T(8,128)(2,1)S(1)} collective-permute-done((bf16[4,2,6,32,128]{4,3,2,1,0:T(8,128)(2,1)S(1)}, bf16[4,2,6,32,128]{4,3,2,1,0:T(8,128)(2,1)S(1)}, u32[]{:S(2)}, u32[]{:S(2)}) %collective-permute-start.4) | collective-permute-done | bytes 393248 | tf_op jit(solution)/shard_map/ppermute | solution.py:737
  34.3 1.9 %collective-permute-start.5 = (bf16[2,2,6,32,128]{4,3,2,1,0:T(8,128)(2,1)S(1)}, bf16[2,2,6,32,128]{4,3,2,1,0:T(8,128)(2,1)S(1)}, u32[]{:S(2)}, u32[]{:S(2)}) collective-permute-start(bf16[2,2,6,32,128]{4,3,2,1,0:T(8,128)(2,1)S(1)} %get-tuple-element.38), channel_id=1, source_target_pairs={{0,0},{1,16},{2,8},{3,24},{4,4},{5,20},{6,12},{7,28},{8,9},{9,25},... | collective-permute-start | bytes 589832 | tf_op jit(solution)/shard_map/ppermute | solution.py:748
  36.2 3.7 %collective-permute-start.6 = (bf16[2,2,6,32,128]{4,3,2,1,0:T(8,128)(2,1)S(1)}, bf16[2,2,6,32,128]{4,3,2,1,0:T(8,128)(2,1)S(1)}, u32[]{:S(2)}, u32[]{:S(2)}) collective-permute-start(bf16[2,2,6,32,128]{4,3,2,1,0:T(8,128)(2,1)S(1)} %get-tuple-element.39), channel_id=1, source_target_pairs={{0,4},{1,20},{2,12},{3,28},{4,0},{5,16},{6,8},{7,24},{8,13},{9,29}... | collective-permute-start | bytes 589832 | tf_op jit(solution)/shard_map/ppermute | solution.py:748
  39.9 3.0 %collective-permute-start.7 = (bf16[2,2,6,32,128]{4,3,2,1,0:T(8,128)(2,1)S(1)}, bf16[2,2,6,32,128]{4,3,2,1,0:T(8,128)(2,1)S(1)}, u32[]{:S(2)}, u32[]{:S(2)}) collective-permute-start(bf16[2,2,6,32,128]{4,3,2,1,0:T(8,128)(2,1)S(1)} %get-tuple-element.40), channel_id=1, source_target_pairs={{0,8},{1,24},{2,0},{3,16},{4,12},{5,28},{6,4},{7,20},{8,1},{9,17},... | collective-permute-start | bytes 589832 | tf_op jit(solution)/shard_map/ppermute | solution.py:748
  42.9 0.1 weights.1.weight_ref
  43.0 7.7 %correlate.1 = f32[4,64,112]{2,1,0:T(8,128)S(1)} custom-call(s32[5]{0:T(128)S(1)} %stack.23.place_ref, bf16[448,6,8,256]{3,2,1,0:T(8,128)(2,1)S(1)} %bitcast.34, bf16[512,1536]{1,0:T(8,128)(2,1)S(1)} %weights.1.weight_ref), custom_call_target="tpu_custom_call" | custom-call | flops 1000000 | bytes 24000000 | tf_op jit(solution)/shard_map/correlate/pallas_call | solution.py:599
  50.7 0.5 collective-permute-start.11
  51.3 1.8 %collective-permute-done.7.refs_2_ = bf16[2,2,6,32,128]{4,3,2,1,0:T(8,128)(2,1)S(1)} collective-permute-done((bf16[2,2,6,32,128]{4,3,2,1,0:T(8,128)(2,1)S(1)}, bf16[2,2,6,32,128]{4,3,2,1,0:T(8,128)(2,1)S(1)}, u32[]{:S(2)}, u32[]{:S(2)}) %collective-permute-start.7) | collective-permute-done | bytes 196640 | tf_op jit(solution)/shard_map/ppermute | solution.py:748
  53.2 0.1 collective-permute-start.10
  53.2 3.8 %collective-permute-start.9 = (f32[64,112]{1,0:T(8,128)S(1)}, f32[64,112]{1,0:T(8,128)S(1)}, u32[]{:S(2)}, u32[]{:S(2)}) collective-permute-start(f32[64,112]{1,0:T(8,128)S(1)} %get-tuple-element.48), channel_id=1, source_target_pairs={{0,2},{1,3},{2,0},{3,1},{4,6},{5,7},{6,4},{7,5},{8,10},{9,11},{10,... | collective-permute-start | bytes 86024 | tf_op jit(solution)/shard_map/ppermute | solution.py:754
  57.0 0.2 order.1.order_ref
  57.2 2.9 %collective-permute-done.11.refs_3_ = bf16[2,2,6,32,128]{4,3,2,1,0:T(8,128)(2,1)S(1)} collective-permute-done((bf16[2,2,6,32,128]{4,3,2,1,0:T(8,128)(2,1)S(1)}, bf16[2,2,6,32,128]{4,3,2,1,0:T(8,128)(2,1)S(1)}, u32[]{:S(2)}, u32[]{:S(2)}) %collective-permute-start.11) | collective-permute-done | bytes 196640 | tf_op jit(solution)/shard_map/ppermute | solution.py:748
  60.2 2.2 %arrange.1 = bf16[2,32,32,192]{3,2,1,0:T(8,128)(2,1)} custom-call(s32[5]{0:T(128)S(1)} %stack.23.place_ref, bf16[512,512]{1,0:T(8,128)(2,1)S(1)} %order.1.order_ref, bf16[2,2,6,32,128]{4,3,2,1,0:T(8,128)(2,1)S(1)} %collective-permute-done.5.refs_0_, bf16[2,2,6,32,128]{4,3,2,1,0:T(8,128)(2,1)S(1)} %collective-permute-done.6.refs_1_, ...), custom_call_target="tpu_custom_call" | custom-call | flops 1000000 | bytes 9000000 | tf_op jit(solution)/shard_map/arrange/pallas_call | solution.py:682
  62.4 0.6 fusion.2
  (18 shorter events, 0.1 us)
Async XLA Ops:
  0.6 6.5 %copy-start.1 = (f32[1,2,3,32,8,256]{5,4,3,2,1,0:T(8,128)S(1)}, f32[1,2,3,32,8,256]{5,4,3,2,1,0:T(8,128)}, u32[]{:S(2)}) copy-start(f32[1,2,3,32,8,256]{5,4,3,2,1,0:T(8,128)} %param.3) | copy-start | bytes 4718596
  0.6 6.5 %copy-start.2 = (f32[1,3,2,3,3,8,256]{6,5,4,3,2,1,0:T(8,128)S(1)}, f32[1,3,2,3,3,8,256]{6,5,4,3,2,1,0:T(8,128)}, u32[]{:S(2)}) copy-start(f32[1,3,2,3,3,8,256]{6,5,4,3,2,1,0:T(8,128)} %param.4) | copy-start | bytes 1327108
  3.5 14.5 %collective-permute-start = (bf16[4,2,6,16,256]{4,3,2,1,0:T(8,128)(2,1)}, bf16[4,2,6,16,256]{4,3,2,1,0:T(8,128)(2,1)S(1)}, u32[]{:S(2)}, u32[]{:S(2)}) collective-permute-start(bf16[4,2,6,16,256]{4,3,2,1,0:T(8,128)(2,1)} %get-tuple-element.24), channel_id=1, source_target_pairs={{0,1},{1,2},{2,3},{3,0},{4,5},{5,6},{6,7},{7,4},{8,9},{9,10},{10,1... | collective-permute-start | bytes 1179656 | tf_op jit(solution)/shard_map/ppermute | solution.py:728
  3.6 14.5 %collective-permute-start.1 = (bf16[4,2,6,16,256]{4,3,2,1,0:T(8,128)(2,1)}, bf16[4,2,6,16,256]{4,3,2,1,0:T(8,128)(2,1)S(1)}, u32[]{:S(2)}, u32[]{:S(2)}) collective-permute-start(bf16[4,2,6,16,256]{4,3,2,1,0:T(8,128)(2,1)} %get-tuple-element.25), channel_id=1, source_target_pairs={{1,0},{2,1},{3,2},{0,3},{5,4},{6,5},{7,6},{4,7},{9,8},{10,9},{11,1... | collective-permute-start | bytes 1179656 | tf_op jit(solution)/shard_map/ppermute | solution.py:729
  5.3 11.6 %collective-permute-start.2 = (bf16[4,54,256]{2,1,0:T(8,128)(2,1)}, bf16[4,54,256]{2,1,0:T(8,128)(2,1)S(1)}, u32[]{:S(2)}, u32[]{:S(2)}) collective-permute-start(bf16[4,54,256]{2,1,0:T(8,128)(2,1)} %get-tuple-element.27), channel_id=1, source_target_pairs={{0,1},{1,2},{2,3},{3,0},{4,5},{5,6},{6,7},{7,4},{8,9},{9,10},{10,1... | collective-permute-start | bytes 331784 | tf_op jit(solution)/shard_map/ppermute | solution.py:726
  5.3 11.6 %collective-permute-start.3 = (bf16[4,54,256]{2,1,0:T(8,128)(2,1)}, bf16[4,54,256]{2,1,0:T(8,128)(2,1)S(1)}, u32[]{:S(2)}, u32[]{:S(2)}) collective-permute-start(bf16[4,54,256]{2,1,0:T(8,128)(2,1)} %get-tuple-element.28), channel_id=1, source_target_pairs={{1,0},{2,1},{3,2},{0,3},{5,4},{6,5},{7,6},{4,7},{9,8},{10,9},{11,1... | collective-permute-start | bytes 331784 | tf_op jit(solution)/shard_map/ppermute | solution.py:727
  18.1 25.0 %copy-start = (bf16[1,448,2,3,8,256]{5,4,3,2,1,0:T(8,128)(2,1)S(1)}, bf16[1,448,2,3,8,256]{5,4,3,2,1,0:T(8,128)(2,1)}, u32[]{:S(2)}) copy-start(bf16[1,448,2,3,8,256]{5,4,3,2,1,0:T(8,128)(2,1)} %param.5) | copy-start | bytes 33030148
  32.2 2.0 %collective-permute-start.4 = (bf16[4,2,6,32,128]{4,3,2,1,0:T(8,128)(2,1)S(1)}, bf16[4,2,6,32,128]{4,3,2,1,0:T(8,128)(2,1)S(1)}, u32[]{:S(2)}, u32[]{:S(2)}) collective-permute-start(bf16[4,2,6,32,128]{4,3,2,1,0:T(8,128)(2,1)S(1)} %get-tuple-element.37), channel_id=1, source_target_pairs={{0,1},{1,0},{2,3},{3,2},{4,5},{5,4},{6,7},{7,6},{8,9},{9,8},{10,11... | collective-permute-start | bytes 1179656 | tf_op jit(solution)/shard_map/ppermute | solution.py:737
  34.3 17.0 %collective-permute-start.5 = (bf16[2,2,6,32,128]{4,3,2,1,0:T(8,128)(2,1)S(1)}, bf16[2,2,6,32,128]{4,3,2,1,0:T(8,128)(2,1)S(1)}, u32[]{:S(2)}, u32[]{:S(2)}) collective-permute-start(bf16[2,2,6,32,128]{4,3,2,1,0:T(8,128)(2,1)S(1)} %get-tuple-element.38), channel_id=1, source_target_pairs={{0,0},{1,16},{2,8},{3,24},{4,4},{5,20},{6,12},{7,28},{8,9},{9,25},... | collective-permute-start | bytes 589832 | tf_op jit(solution)/shard_map/ppermute | solution.py:748
  36.2 15.1 %collective-permute-start.6 = (bf16[2,2,6,32,128]{4,3,2,1,0:T(8,128)(2,1)S(1)}, bf16[2,2,6,32,128]{4,3,2,1,0:T(8,128)(2,1)S(1)}, u32[]{:S(2)}, u32[]{:S(2)}) collective-permute-start(bf16[2,2,6,32,128]{4,3,2,1,0:T(8,128)(2,1)S(1)} %get-tuple-element.39), channel_id=1, source_target_pairs={{0,4},{1,20},{2,12},{3,28},{4,0},{5,16},{6,8},{7,24},{8,13},{9,29}... | collective-permute-start | bytes 589832 | tf_op jit(solution)/shard_map/ppermute | solution.py:748
  39.9 13.2 %collective-permute-start.7 = (bf16[2,2,6,32,128]{4,3,2,1,0:T(8,128)(2,1)S(1)}, bf16[2,2,6,32,128]{4,3,2,1,0:T(8,128)(2,1)S(1)}, u32[]{:S(2)}, u32[]{:S(2)}) collective-permute-start(bf16[2,2,6,32,128]{4,3,2,1,0:T(8,128)(2,1)S(1)} %get-tuple-element.40), channel_id=1, source_target_pairs={{0,8},{1,24},{2,0},{3,16},{4,12},{5,28},{6,4},{7,20},{8,1},{9,17},... | collective-permute-start | bytes 589832 | tf_op jit(solution)/shard_map/ppermute | solution.py:748
  50.7 9.4 %collective-permute-start.11 = (bf16[2,2,6,32,128]{4,3,2,1,0:T(8,128)(2,1)S(1)}, bf16[2,2,6,32,128]{4,3,2,1,0:T(8,128)(2,1)S(1)}, u32[]{:S(2)}, u32[]{:S(2)}) collective-permute-start(bf16[2,2,6,32,128]{4,3,2,1,0:T(8,128)(2,1)S(1)} %get-tuple-element.45), channel_id=1, source_target_pairs={{0,12},{1,28},{2,4},{3,20},{4,8},{5,24},{6,0},{7,16},{8,5},{9,21},... | collective-permute-start | bytes 589832 | tf_op jit(solution)/shard_map/ppermute | solution.py:748
  53.2 9.2 %collective-permute-start.10 = (f32[64,112]{1,0:T(8,128)S(1)}, f32[64,112]{1,0:T(8,128)S(1)}, u32[]{:S(2)}, u32[]{:S(2)}) collective-permute-start(f32[64,112]{1,0:T(8,128)S(1)} %get-tuple-element.47), channel_id=1, source_target_pairs={{0,3},{1,2},{2,1},{3,0},{4,7},{5,6},{6,5},{7,4},{8,11},{9,10},{10,... | collective-permute-start | bytes 86024 | tf_op jit(solution)/shard_map/ppermute | solution.py:754
  53.2 9.1 %collective-permute-start.9 = (f32[64,112]{1,0:T(8,128)S(1)}, f32[64,112]{1,0:T(8,128)S(1)}, u32[]{:S(2)}, u32[]{:S(2)}) collective-permute-start(f32[64,112]{1,0:T(8,128)S(1)} %get-tuple-element.48), channel_id=1, source_target_pairs={{0,2},{1,3},{2,0},{3,1},{4,6},{5,7},{6,4},{7,5},{8,10},{9,11},{10,... | collective-permute-start | bytes 86024 | tf_op jit(solution)/shard_map/ppermute | solution.py:754
  57.0 5.4 %collective-permute-start.8 = (f32[64,112]{1,0:T(8,128)S(1)}, f32[64,112]{1,0:T(8,128)S(1)}, u32[]{:S(2)}, u32[]{:S(2)}) collective-permute-start(f32[64,112]{1,0:T(8,128)S(1)} %get-tuple-element.46), channel_id=1, source_target_pairs={{0,1},{1,0},{2,3},{3,2},{4,5},{5,4},{6,7},{7,6},{8,9},{9,8},{10,11... | collective-permute-start | bytes 86024 | tf_op jit(solution)/shard_map/ppermute | solution.py:754

commit v5 on v4

--- a/solution.py
+++ b/solution.py
@@ -476,20 +476,19 @@
     src, prev = (a_ref, b_ref) if DEGREE % 2 else (b_ref, a_ref)
 
     def last(n, _):
-        g, at = n // (layers // 4), n % (layers // 4)
-        for u in range(4):
-            x = 4 * at + u
+        g = n
+        for x in range(layers):
             value = layer(table_ref, g, x + DEGREE, src, prev, False, tiles)
             value = turn(gauge_ref, x + DEGREE, lambda k, t: value[k, t], True, tiles)
             for (k, t), v in value.items():
                 rounded = v.astype(jnp.bfloat16)
                 half_ref[g, x, k, :, cols(t)] = rounded
-                pack_ref[g, k, pl.ds(pl.multiple_of(x * VB, VB), VB), cols(t)] = rounded.astype(
+                pack_ref[g, k, pl.ds(x * VB, VB), cols(t)] = rounded.astype(
                     jnp.float32
                 )
         return 0
 
-    lax.fori_loop(0, groups * (layers // 4), last, 0)
+    lax.fori_loop(0, groups, last, 0)
 
     side, base = place_ref[0], place_ref[1]
     pairs = parts // 2

time: 64.1 us -> 64 us (level)
  no operation moved by 1% of the time
where the time goes in v5:
time: 64 us; the launch traced here: 62.8 us
  Pallas kernels  36.3 us (57%)
  starting transfers between devices  17.2 us (27%)
  waiting for transfers between devices  7.9 us (12%)
  between operations  0.77 us (1%)
    pallas_call x1, Pallas kernels, run_outer(): pl.pallas_call(functools.partial(outer_kernel, layers=layers, parts=parts...  14 us
    ppermute x4, starting transfers between devices, shards(): sent[step] = lax.ppermute(blocks[step], ('tm', 'space'), table_of)  9.14 us
    pallas_call x1, Pallas kernels, run_inner(): pl.pallas_call(functools.partial(inner_kernel, layers=layers), in_specs=[...  7.96 us
    pallas_call x1, Pallas kernels, run_corr(): pl.pallas_call(functools.partial(corr_kernel, layers=layers), grid_spec=g...  7.7 us
    ppermute x4, waiting for transfers between devices, shards(): sent[step] = lax.ppermute(blocks[step], ('tm', 'space'), table_of)  4.79 us
    ppermute x3, starting transfers between devices, shards(): total = total + lax.ppermute(partial[distance], 'space', partner)  3.83 us
    pallas_call x1, Pallas kernels, run_pack(): pl.pallas_call(functools.partial(pack_kernel, layers=layers, tiles=tiles)...  2.85 us
    pallas_call x1, Pallas kernels, run_arrange(): pl.pallas_call(functools.partial(arrange_kernel, layers=layers, per=per),...  2.16 us
  transfers between devices with their start and end apart: 12, of which 4 were waited for; matrix products, arithmetic and copies ran while one was open for 0% of the time, Pallas kernels for 31%

profile of v5, /device:TPU:12, one launch (start us, length us, event | category | flops | bytes accessed | tf_op | source)
XLA Modules:
  0.0 62.8 jit_solution(5758397964409127545)
XLA Ops:
  0.6 2.8 %pack.1 = (bf16[4,54,256]{2,1,0:T(8,128)(2,1)}, bf16[4,54,256]{2,1,0:T(8,128)(2,1)}, bf16[4,2,6,16,256]{4,3,2,1,0:T(8,128)(2,1)}, bf16[4,2,6,16,256]{4,3,2,1,0:T(8,128)(2,1)}) custom-call(f32[6,512,128]{2,1,0:T(8,128)} %bitcast.35, f32[864,128]{1,0:T(8,128)} %bitcast.37), custom_call_target="tpu_custom_call" | custom-call | flops 1000000 | bytes 7500000 | tf_op jit(solution)/shard_map/pack/pallas_call | solution.py:98
  3.5 0.1 collective-permute-start
  3.6 1.7 %collective-permute-start.1 = (bf16[4,2,6,16,256]{4,3,2,1,0:T(8,128)(2,1)}, bf16[4,2,6,16,256]{4,3,2,1,0:T(8,128)(2,1)S(1)}, u32[]{:S(2)}, u32[]{:S(2)}) collective-permute-start(bf16[4,2,6,16,256]{4,3,2,1,0:T(8,128)(2,1)} %get-tuple-element.25), channel_id=1, source_target_pairs={{1,0},{2,1},{3,2},{0,3},{5,4},{6,5},{7,6},{4,7},{9,8},{10,9},{11,1... | collective-permute-start | bytes 1179656 | tf_op jit(solution)/shard_map/ppermute | solution.py:728
  5.3 1.7 %collective-permute-start.3 = (bf16[4,54,256]{2,1,0:T(8,128)(2,1)}, bf16[4,54,256]{2,1,0:T(8,128)(2,1)S(1)}, u32[]{:S(2)}, u32[]{:S(2)}) collective-permute-start(bf16[4,54,256]{2,1,0:T(8,128)(2,1)} %get-tuple-element.28), channel_id=1, source_target_pairs={{1,0},{2,1},{3,2},{0,3},{5,4},{6,5},{7,6},{4,7},{9,8},{10,9},{11,1... | collective-permute-start | bytes 331784 | tf_op jit(solution)/shard_map/ppermute | solution.py:726
  7.1 0.1 stack.23.place_ref
  7.1 8.0 %inner.1 = (f32[2,16,6,16,256]{4,3,2,1,0:T(8,128)S(1)}, f32[2,16,6,16,256]{4,3,2,1,0:T(8,128)S(1)}, f32[16,112,256]{2,1,0:T(8,128)S(1)}, f32[16,24,256]{2,1,0:T(8,128)S(1)}, f32[24,256]{1,0:T(8,128)S(1)}) custom-call(f32[6,512,128]{2,1,0:T(8,128)S(1)} %bitcast.36, f32[864,128]{1,0:T(8,128)S(1)} %bitcast.38), custom_call_target="tpu_custom_call" | custom-call | flops 1000000 | bytes 24000000 | tf_op jit(solution)/shard_map/inner/pallas_call | solution.py:431
  15.1 1.8 %collective-permute-done.2.lo_ref = bf16[4,54,256]{2,1,0:T(8,128)(2,1)S(1)} collective-permute-done((bf16[4,54,256]{2,1,0:T(8,128)(2,1)}, bf16[4,54,256]{2,1,0:T(8,128)(2,1)S(1)}, u32[]{:S(2)}, u32[]{:S(2)}) %collective-permute-start.2) | collective-permute-done | bytes 110624 | tf_op jit(solution)/shard_map/ppermute | solution.py:725
  16.9 1.2 %gauge_halo.1 = (f32[16,112,256]{2,1,0:T(8,128)S(1)}, f32[16,24,256]{2,1,0:T(8,128)S(1)}) custom-call(f32[24,256]{1,0:T(8,128)S(1)} %get-tuple-element.26.top_ref, bf16[4,54,256]{2,1,0:T(8,128)(2,1)S(1)} %collective-permute-done.2.lo_ref, bf16[4,54,256]{2,1,0:T(8,128)(2,1)S(1)} %collective-permute-done.3.hi_ref, ...), custom_call_target="tpu_custom_call" | custom-call | flops 1000000 | bytes 4500000 | tf_op jit(solution)/shard_map/gauge_halo/pallas_call | solution.py:288
  18.1 14.0 %outer.1 = (bf16[2,8,6,16,256]{4,3,2,1,0:T(8,128)(2,1)S(1)}, bf16[4,2,6,32,128]{4,3,2,1,0:T(8,128)(2,1)S(1)}, bf16[4,2,6,32,128]{4,3,2,1,0:T(8,128)(2,1)S(1)}) custom-call(s32[5]{0:T(128)S(1)} %stack.23.place_ref, bf16[4,2,6,16,256]{4,3,2,1,0:T(8,128)(2,1)S(1)} %collective-permute-done.lo_ref, bf16[4,2,6,16,256]{4,3,2,1,0:T(8,128)(2,1)S(1)} %collective-permute-done.1.hi_ref, ...), custom_call_target="tpu_custom_call" | custom-call | flops 1000000 | bytes 48000000 | tf_op jit(solution)/shard_map/outer/pallas_call | solution.py:512
  32.1 0.7 %collective-permute-start.4 = (bf16[4,2,6,32,128]{4,3,2,1,0:T(8,128)(2,1)S(1)}, bf16[4,2,6,32,128]{4,3,2,1,0:T(8,128)(2,1)S(1)}, u32[]{:S(2)}, u32[]{:S(2)}) collective-permute-start(bf16[4,2,6,32,128]{4,3,2,1,0:T(8,128)(2,1)S(1)} %get-tuple-element.37), channel_id=1, source_target_pairs={{0,1},{1,0},{2,3},{3,2},{4,5},{5,4},{6,7},{7,6},{8,9},{9,8},{10,11... | collective-permute-start | bytes 1179656 | tf_op jit(solution)/shard_map/ppermute | solution.py:736
  32.8 1.3 %collective-permute-done.4.got_ref = bf16[4,2,6,32,128]{4,3,2,1,0:T(8,128)(2,1)S(1)} collective-permute-done((bf16[4,2,6,32,128]{4,3,2,1,0:T(8,128)(2,1)S(1)}, bf16[4,2,6,32,128]{4,3,2,1,0:T(8,128)(2,1)S(1)}, u32[]{:S(2)}, u32[]{:S(2)}) %collective-permute-start.4) | collective-permute-done | bytes 393248 | tf_op jit(solution)/shard_map/ppermute | solution.py:736
  34.2 1.9 %collective-permute-start.5 = (bf16[2,2,6,32,128]{4,3,2,1,0:T(8,128)(2,1)S(1)}, bf16[2,2,6,32,128]{4,3,2,1,0:T(8,128)(2,1)S(1)}, u32[]{:S(2)}, u32[]{:S(2)}) collective-permute-start(bf16[2,2,6,32,128]{4,3,2,1,0:T(8,128)(2,1)S(1)} %get-tuple-element.38), channel_id=1, source_target_pairs={{0,0},{1,16},{2,8},{3,24},{4,4},{5,20},{6,12},{7,28},{8,9},{9,25},... | collective-permute-start | bytes 589832 | tf_op jit(solution)/shard_map/ppermute | solution.py:747
  36.1 3.7 %collective-permute-start.6 = (bf16[2,2,6,32,128]{4,3,2,1,0:T(8,128)(2,1)S(1)}, bf16[2,2,6,32,128]{4,3,2,1,0:T(8,128)(2,1)S(1)}, u32[]{:S(2)}, u32[]{:S(2)}) collective-permute-start(bf16[2,2,6,32,128]{4,3,2,1,0:T(8,128)(2,1)S(1)} %get-tuple-element.39), channel_id=1, source_target_pairs={{0,4},{1,20},{2,12},{3,28},{4,0},{5,16},{6,8},{7,24},{8,13},{9,29}... | collective-permute-start | bytes 589832 | tf_op jit(solution)/shard_map/ppermute | solution.py:747
  39.8 3.0 %collective-permute-start.7 = (bf16[2,2,6,32,128]{4,3,2,1,0:T(8,128)(2,1)S(1)}, bf16[2,2,6,32,128]{4,3,2,1,0:T(8,128)(2,1)S(1)}, u32[]{:S(2)}, u32[]{:S(2)}) collective-permute-start(bf16[2,2,6,32,128]{4,3,2,1,0:T(8,128)(2,1)S(1)} %get-tuple-element.40), channel_id=1, source_target_pairs={{0,8},{1,24},{2,0},{3,16},{4,12},{5,28},{6,4},{7,20},{8,1},{9,17},... | collective-permute-start | bytes 589832 | tf_op jit(solution)/shard_map/ppermute | solution.py:747
  42.8 0.1 weights.1.weight_ref
  42.9 7.7 %correlate.1 = f32[4,64,112]{2,1,0:T(8,128)S(1)} custom-call(s32[5]{0:T(128)S(1)} %stack.23.place_ref, bf16[448,6,8,256]{3,2,1,0:T(8,128)(2,1)S(1)} %bitcast.34, bf16[512,1536]{1,0:T(8,128)(2,1)S(1)} %weights.1.weight_ref), custom_call_target="tpu_custom_call" | custom-call | flops 1000000 | bytes 24000000 | tf_op jit(solution)/shard_map/correlate/pallas_call | solution.py:598
  50.6 0.5 collective-permute-start.11
  51.2 1.8 %collective-permute-done.7.refs_2_ = bf16[2,2,6,32,128]{4,3,2,1,0:T(8,128)(2,1)S(1)} collective-permute-done((bf16[2,2,6,32,128]{4,3,2,1,0:T(8,128)(2,1)S(1)}, bf16[2,2,6,32,128]{4,3,2,1,0:T(8,128)(2,1)S(1)}, u32[]{:S(2)}, u32[]{:S(2)}) %collective-permute-start.7) | collective-permute-done | bytes 196640 | tf_op jit(solution)/shard_map/ppermute | solution.py:747
  53.0 0.1 collective-permute-start.10
  53.1 3.8 %collective-permute-start.9 = (f32[64,112]{1,0:T(8,128)S(1)}, f32[64,112]{1,0:T(8,128)S(1)}, u32[]{:S(2)}, u32[]{:S(2)}) collective-permute-start(f32[64,112]{1,0:T(8,128)S(1)} %get-tuple-element.48), channel_id=1, source_target_pairs={{0,2},{1,3},{2,0},{3,1},{4,6},{5,7},{6,4},{7,5},{8,10},{9,11},{10,... | collective-permute-start | bytes 86024 | tf_op jit(solution)/shard_map/ppermute | solution.py:753
  56.9 0.2 order.1.order_ref
  57.1 2.9 %collective-permute-done.11.refs_3_ = bf16[2,2,6,32,128]{4,3,2,1,0:T(8,128)(2,1)S(1)} collective-permute-done((bf16[2,2,6,32,128]{4,3,2,1,0:T(8,128)(2,1)S(1)}, bf16[2,2,6,32,128]{4,3,2,1,0:T(8,128)(2,1)S(1)}, u32[]{:S(2)}, u32[]{:S(2)}) %collective-permute-start.11) | collective-permute-done | bytes 196640 | tf_op jit(solution)/shard_map/ppermute | solution.py:747
  60.0 2.2 %arrange.1 = bf16[2,32,32,192]{3,2,1,0:T(8,128)(2,1)} custom-call(s32[5]{0:T(128)S(1)} %stack.23.place_ref, bf16[512,512]{1,0:T(8,128)(2,1)S(1)} %order.1.order_ref, bf16[2,2,6,32,128]{4,3,2,1,0:T(8,128)(2,1)S(1)} %collective-permute-done.5.refs_0_, bf16[2,2,6,32,128]{4,3,2,1,0:T(8,128)(2,1)S(1)} %collective-permute-done.6.refs_1_, ...), custom_call_target="tpu_custom_call" | custom-call | flops 1000000 | bytes 9000000 | tf_op jit(solution)/shard_map/arrange/pallas_call | solution.py:681
  62.2 0.6 fusion.2
  (18 shorter events, 0.1 us)
Async XLA Ops:
  0.6 6.5 %copy-start.1 = (f32[1,2,3,32,8,256]{5,4,3,2,1,0:T(8,128)S(1)}, f32[1,2,3,32,8,256]{5,4,3,2,1,0:T(8,128)}, u32[]{:S(2)}) copy-start(f32[1,2,3,32,8,256]{5,4,3,2,1,0:T(8,128)} %param.3) | copy-start | bytes 4718596
  0.6 6.5 %copy-start.2 = (f32[1,3,2,3,3,8,256]{6,5,4,3,2,1,0:T(8,128)S(1)}, f32[1,3,2,3,3,8,256]{6,5,4,3,2,1,0:T(8,128)}, u32[]{:S(2)}) copy-start(f32[1,3,2,3,3,8,256]{6,5,4,3,2,1,0:T(8,128)} %param.4) | copy-start | bytes 1327108
  3.5 14.5 %collective-permute-start = (bf16[4,2,6,16,256]{4,3,2,1,0:T(8,128)(2,1)}, bf16[4,2,6,16,256]{4,3,2,1,0:T(8,128)(2,1)S(1)}, u32[]{:S(2)}, u32[]{:S(2)}) collective-permute-start(bf16[4,2,6,16,256]{4,3,2,1,0:T(8,128)(2,1)} %get-tuple-element.24), channel_id=1, source_target_pairs={{0,1},{1,2},{2,3},{3,0},{4,5},{5,6},{6,7},{7,4},{8,9},{9,10},{10,1... | collective-permute-start | bytes 1179656 | tf_op jit(solution)/shard_map/ppermute | solution.py:727
  3.6 14.5 %collective-permute-start.1 = (bf16[4,2,6,16,256]{4,3,2,1,0:T(8,128)(2,1)}, bf16[4,2,6,16,256]{4,3,2,1,0:T(8,128)(2,1)S(1)}, u32[]{:S(2)}, u32[]{:S(2)}) collective-permute-start(bf16[4,2,6,16,256]{4,3,2,1,0:T(8,128)(2,1)} %get-tuple-element.25), channel_id=1, source_target_pairs={{1,0},{2,1},{3,2},{0,3},{5,4},{6,5},{7,6},{4,7},{9,8},{10,9},{11,1... | collective-permute-start | bytes 1179656 | tf_op jit(solution)/shard_map/ppermute | solution.py:728
  5.3 11.6 %collective-permute-start.2 = (bf16[4,54,256]{2,1,0:T(8,128)(2,1)}, bf16[4,54,256]{2,1,0:T(8,128)(2,1)S(1)}, u32[]{:S(2)}, u32[]{:S(2)}) collective-permute-start(bf16[4,54,256]{2,1,0:T(8,128)(2,1)} %get-tuple-element.27), channel_id=1, source_target_pairs={{0,1},{1,2},{2,3},{3,0},{4,5},{5,6},{6,7},{7,4},{8,9},{9,10},{10,1... | collective-permute-start | bytes 331784 | tf_op jit(solution)/shard_map/ppermute | solution.py:725
  5.3 11.6 %collective-permute-start.3 = (bf16[4,54,256]{2,1,0:T(8,128)(2,1)}, bf16[4,54,256]{2,1,0:T(8,128)(2,1)S(1)}, u32[]{:S(2)}, u32[]{:S(2)}) collective-permute-start(bf16[4,54,256]{2,1,0:T(8,128)(2,1)} %get-tuple-element.28), channel_id=1, source_target_pairs={{1,0},{2,1},{3,2},{0,3},{5,4},{6,5},{7,6},{4,7},{9,8},{10,9},{11,1... | collective-permute-start | bytes 331784 | tf_op jit(solution)/shard_map/ppermute | solution.py:726
  18.1 24.8 %copy-start = (bf16[1,448,2,3,8,256]{5,4,3,2,1,0:T(8,128)(2,1)S(1)}, bf16[1,448,2,3,8,256]{5,4,3,2,1,0:T(8,128)(2,1)}, u32[]{:S(2)}) copy-start(bf16[1,448,2,3,8,256]{5,4,3,2,1,0:T(8,128)(2,1)} %param.5) | copy-start | bytes 33030148
  32.1 2.0 %collective-permute-start.4 = (bf16[4,2,6,32,128]{4,3,2,1,0:T(8,128)(2,1)S(1)}, bf16[4,2,6,32,128]{4,3,2,1,0:T(8,128)(2,1)S(1)}, u32[]{:S(2)}, u32[]{:S(2)}) collective-permute-start(bf16[4,2,6,32,128]{4,3,2,1,0:T(8,128)(2,1)S(1)} %get-tuple-element.37), channel_id=1, source_target_pairs={{0,1},{1,0},{2,3},{3,2},{4,5},{5,4},{6,7},{7,6},{8,9},{9,8},{10,11... | collective-permute-start | bytes 1179656 | tf_op jit(solution)/shard_map/ppermute | solution.py:736
  34.2 17.0 %collective-permute-start.5 = (bf16[2,2,6,32,128]{4,3,2,1,0:T(8,128)(2,1)S(1)}, bf16[2,2,6,32,128]{4,3,2,1,0:T(8,128)(2,1)S(1)}, u32[]{:S(2)}, u32[]{:S(2)}) collective-permute-start(bf16[2,2,6,32,128]{4,3,2,1,0:T(8,128)(2,1)S(1)} %get-tuple-element.38), channel_id=1, source_target_pairs={{0,0},{1,16},{2,8},{3,24},{4,4},{5,20},{6,12},{7,28},{8,9},{9,25},... | collective-permute-start | bytes 589832 | tf_op jit(solution)/shard_map/ppermute | solution.py:747
  36.1 15.1 %collective-permute-start.6 = (bf16[2,2,6,32,128]{4,3,2,1,0:T(8,128)(2,1)S(1)}, bf16[2,2,6,32,128]{4,3,2,1,0:T(8,128)(2,1)S(1)}, u32[]{:S(2)}, u32[]{:S(2)}) collective-permute-start(bf16[2,2,6,32,128]{4,3,2,1,0:T(8,128)(2,1)S(1)} %get-tuple-element.39), channel_id=1, source_target_pairs={{0,4},{1,20},{2,12},{3,28},{4,0},{5,16},{6,8},{7,24},{8,13},{9,29}... | collective-permute-start | bytes 589832 | tf_op jit(solution)/shard_map/ppermute | solution.py:747
  39.8 13.2 %collective-permute-start.7 = (bf16[2,2,6,32,128]{4,3,2,1,0:T(8,128)(2,1)S(1)}, bf16[2,2,6,32,128]{4,3,2,1,0:T(8,128)(2,1)S(1)}, u32[]{:S(2)}, u32[]{:S(2)}) collective-permute-start(bf16[2,2,6,32,128]{4,3,2,1,0:T(8,128)(2,1)S(1)} %get-tuple-element.40), channel_id=1, source_target_pairs={{0,8},{1,24},{2,0},{3,16},{4,12},{5,28},{6,4},{7,20},{8,1},{9,17},... | collective-permute-start | bytes 589832 | tf_op jit(solution)/shard_map/ppermute | solution.py:747
  50.6 9.4 %collective-permute-start.11 = (bf16[2,2,6,32,128]{4,3,2,1,0:T(8,128)(2,1)S(1)}, bf16[2,2,6,32,128]{4,3,2,1,0:T(8,128)(2,1)S(1)}, u32[]{:S(2)}, u32[]{:S(2)}) collective-permute-start(bf16[2,2,6,32,128]{4,3,2,1,0:T(8,128)(2,1)S(1)} %get-tuple-element.45), channel_id=1, source_target_pairs={{0,12},{1,28},{2,4},{3,20},{4,8},{5,24},{6,0},{7,16},{8,5},{9,21},... | collective-permute-start | bytes 589832 | tf_op jit(solution)/shard_map/ppermute | solution.py:747
  53.0 9.2 %collective-permute-start.10 = (f32[64,112]{1,0:T(8,128)S(1)}, f32[64,112]{1,0:T(8,128)S(1)}, u32[]{:S(2)}, u32[]{:S(2)}) collective-permute-start(f32[64,112]{1,0:T(8,128)S(1)} %get-tuple-element.47), channel_id=1, source_target_pairs={{0,3},{1,2},{2,1},{3,0},{4,7},{5,6},{6,5},{7,4},{8,11},{9,10},{10,... | collective-permute-start | bytes 86024 | tf_op jit(solution)/shard_map/ppermute | solution.py:753
  53.1 9.1 %collective-permute-start.9 = (f32[64,112]{1,0:T(8,128)S(1)}, f32[64,112]{1,0:T(8,128)S(1)}, u32[]{:S(2)}, u32[]{:S(2)}) collective-permute-start(f32[64,112]{1,0:T(8,128)S(1)} %get-tuple-element.48), channel_id=1, source_target_pairs={{0,2},{1,3},{2,0},{3,1},{4,6},{5,7},{6,4},{7,5},{8,10},{9,11},{10,... | collective-permute-start | bytes 86024 | tf_op jit(solution)/shard_map/ppermute | solution.py:753
  56.8 5.4 %collective-permute-start.8 = (f32[64,112]{1,0:T(8,128)S(1)}, f32[64,112]{1,0:T(8,128)S(1)}, u32[]{:S(2)}, u32[]{:S(2)}) collective-permute-start(f32[64,112]{1,0:T(8,128)S(1)} %get-tuple-element.46), channel_id=1, source_target_pairs={{0,1},{1,0},{2,3},{3,2},{4,5},{5,4},{6,7},{7,6},{8,9},{9,8},{10,11... | collective-permute-start | bytes 86024 | tf_op jit(solution)/shard_map/ppermute | solution.py:753
